TPU v7x, 256 devices: a whole 4x4x8 slice. The times are simulated.
256 devices in a mesh: sup: 32 (over x, z), tm: 8 (over y, core).
Axes of the slice: x: 4, y: 4, z: 8, core: 2. Of those that a mesh axis runs over, the one named last changes fastest.
Arguments:
- factor: bfloat16 [8192, 8192], P('sup'), may hold values from -6 to 6, as said below
- white_noise: bfloat16 [8192, 16384], P('sup', 'tm'), may hold values from -6 to 6
- site_class: int32 [8192], replicated, may hold values from 0 to 3
- site_decay: float32 [2, 4], replicated, may hold values from 2e-05 to 0.02
- site_angle: float32 [2, 4], replicated, may hold values from 0.05 to 0.8
- site_mix: float32 [4, 4], replicated, may hold values from -3 to 3
Outputs:
- motions: float32 [8192, 16384], P('sup', 'tm')
Inputs may be any that keep to these rules, and one draw needn't show every extreme that they name: factor is zero above the diagonal and one on it.
All inputs are finite; a program needn't handle non-finite values.
Results may differ from a plain program's by a relative error of at most 0.0045.
Values may be sent and summed in bfloat16 or wider, within the bound.
No kernel may reach another device: no remote copies, remote signals or barrier semaphores. Data moves between devices by JAX's collectives and lax.ppermute only.
A program may use at most 128 MiB of HBM per device.

v0:
```python
import jax
import jax.numpy as jnp
from jax import lax
from jax.sharding import PartitionSpec as P

CH = 256


PRECISE = lax.Precision.HIGHEST


def passed_along(value, axis, by):
    size = lax.axis_size(axis)
    pairs = [(i, i + by) for i in range(size) if 0 <= i + by < size]
    return lax.ppermute(value, axis, pairs)


def system(site_decay, site_angle, site_mix):
    radius = 1.0 - site_decay
    norm_gain = jnp.sqrt(site_decay * (2.0 - site_decay))
    cos_ground = radius[0] * jnp.cos(site_angle[0])
    sin_ground = radius[0] * jnp.sin(site_angle[0])
    cos_high = radius[1] * jnp.cos(site_angle[1])
    sin_high = radius[1] * jnp.sin(site_angle[1])
    zeros_row = jnp.zeros_like(cos_ground)
    ones_row = jnp.ones_like(cos_ground)
    mix_a, mix_b, out_a, out_b = (site_mix[0], site_mix[1], site_mix[2], site_mix[3])
    row_list = [
        [cos_ground, -sin_ground, zeros_row, zeros_row],
        [sin_ground, cos_ground, zeros_row, zeros_row],
        [
            norm_gain[0] * (mix_a * cos_ground + mix_b * sin_ground),
            norm_gain[0] * (mix_b * cos_ground - mix_a * sin_ground),
            cos_high,
            -sin_high,
        ],
        [zeros_row, zeros_row, sin_high, cos_high],
    ]
    matrix = jnp.stack([jnp.stack(entries, axis=-1) for entries in row_list], axis=1)
    entry_vec = jnp.stack([ones_row, zeros_row, norm_gain[0] * mix_a, zeros_row], axis=-1)
    readout = jnp.stack([zeros_row, zeros_row, norm_gain[1] * out_a, norm_gain[1] * out_b], axis=-1)
    return (matrix, entry_vec, readout)


def power_table(matrix, length_total):
    powers = matrix[None]
    while powers.shape[0] < length_total:
        top_power = powers[-1]
        further = jnp.einsum("kab,jkbc->jkac", top_power, powers, precision=PRECISE)
        powers = jnp.concatenate([powers, further], axis=0)
    return (powers[-1], powers)


def tables(site_decay, site_angle, site_mix, length_total, group_len):
    matrix, entry_vec, readout = system(site_decay, site_angle, site_mix)
    classes = matrix.shape[0]
    block_power, powers = power_table(matrix, max(length_total, group_len))
    gains = jnp.einsum("ka,jkab->kbj", readout, powers, precision=PRECISE)
    responses = jnp.einsum("jkab,kb->kja", powers[: group_len - 1], entry_vec, precision=PRECISE)
    responses = jnp.concatenate([entry_vec[:, None, :], responses], axis=1)
    impulse = jnp.einsum("ka,kma->km", readout, responses, precision=PRECISE)
    padded_len = 2 * group_len
    padded = jnp.concatenate([impulse, jnp.zeros((classes, group_len), jnp.float32)], axis=1)
    tiled = jnp.tile(padded, (1, group_len))[:, : group_len * (padded_len - 1)]
    toeplitz = tiled.reshape(classes, group_len, padded_len - 1)[:, :, :group_len]
    toeplitz_cat = (
        toeplitz.transpose(1, 0, 2).reshape(group_len, classes * group_len).astype(jnp.bfloat16)
    )
    final_cat = (
        responses[:, ::-1, :]
        .transpose(1, 0, 2)
        .reshape(group_len, classes * 4)
        .astype(jnp.bfloat16)
    )
    group_power = powers[group_len - 1]
    return (toeplitz_cat, gains, final_cat, group_power, powers[length_total - 1])


def filter_group(group_input, onehot, toeplitz_cat, gain_rows, power_rows, final_cat, carry_state):
    row_count = group_input.shape[0]
    group_len = group_input.shape[1]
    classes = onehot.shape[1]
    all_classes = jnp.dot(group_input, toeplitz_cat, preferred_element_type=jnp.float32).reshape(
        row_count, classes, group_len
    )
    filtered = jnp.sum(onehot[:, :, None] * all_classes, axis=1)
    filtered = filtered + jnp.einsum("rcj,cr->rj", gain_rows, carry_state, precision=PRECISE)
    entered = jnp.dot(group_input, final_cat, preferred_element_type=jnp.float32).reshape(
        row_count, classes, 4
    )
    entered = jnp.sum(onehot[:, :, None] * entered, axis=1)
    carry_state = jnp.einsum("rca,ar->cr", power_rows, carry_state, precision=PRECISE) + entered.T
    return (filtered, carry_state)


def add_piece(running, left_rows, piece_rows, first_index, col_limit):

    def product(partial_sum):
        return jnp.dot(left_rows, piece_rows, preferred_element_type=jnp.float32)

    def unchanged(partial_sum):
        return partial_sum

    return lax.cond(first_index < col_limit, product, unchanged, running)


def body(factor, white_noise, site_class, site_decay, site_angle, site_mix):
    row_count = factor.shape[0]
    time_span = white_noise.shape[1]
    classes = site_decay.shape[1]
    my_index = lax.axis_index("sup")
    first_row = my_index * row_count
    own_limit = first_row + row_count
    summed = add_piece(
        jnp.zeros((row_count, time_span), jnp.float32),
        factor,
        lax.all_gather(white_noise, "sup", axis=0, tiled=True),
        jnp.int32(0),
        own_limit,
    )
    row_class = lax.dynamic_slice_in_dim(site_class, first_row, row_count)
    excitation = summed.astype(jnp.bfloat16)
    onehot = (row_class[:, None] == jnp.arange(classes, dtype=jnp.int32)[None, :]).astype(
        jnp.float32
    )
    toeplitz_cat, gains, final_cat, group_power, block_power = tables(
        site_decay, site_angle, site_mix, time_span, CH
    )
    gain_rows = jnp.einsum("rk,kcj->rcj", onehot, gains[:, :, :CH], precision=PRECISE)
    power_rows = jnp.einsum("rk,kab->rab", onehot, group_power, precision=PRECISE)
    carry_state = jnp.zeros((4, row_count), jnp.float32)
    pieces = []
    for position in range(time_span // CH):
        filtered, carry_state = filter_group(
            excitation[:, position * CH : (position + 1) * CH],
            onehot,
            toeplitz_cat,
            gain_rows,
            power_rows,
            final_cat,
            carry_state,
        )
        pieces.append(filtered)
    local_part = jnp.concatenate(pieces, axis=1)
    block_rows = jnp.einsum("rk,kab->abr", onehot, block_power, precision=PRECISE)

    def relay(counter, incoming_state):
        advanced = (
            jnp.einsum("abr,br->ar", block_rows, incoming_state, precision=PRECISE) + carry_state
        )
        return passed_along(advanced, "tm", 1)

    incoming = lax.fori_loop(
        0, lax.axis_size("tm") - 1, relay, jnp.zeros((4, row_count), jnp.float32)
    )
    gain_block = jnp.einsum("rk,kcj->rcj", onehot, gains, precision=PRECISE)
    motions = local_part + jnp.einsum("rcj,cr->rj", gain_block, incoming, precision=PRECISE)
    return motions


def solution(mesh):
    in_specs = (P("sup", None), P("sup", "tm"), P(), P(), P(), P())
    out_specs = P("sup", "tm")
    return jax.shard_map(body, mesh=mesh, in_specs=in_specs, out_specs=out_specs, check_vma=False)
```

profile of v0, /device:TPU:1, one launch (start us, length us, event | category | flops | bytes accessed | tf_op | source)
XLA Modules:
  0.0 360.8 jit_solution(5074133898657482796)
XLA Ops:
  6.5 0.7 all-gather.2.cloned.1.call-update
  7.3 0.7 broadcast_subtract_fusion
  7.9 0.7 fusion.112
  8.8 0.8 multiply_bitcast_fusion.5
  9.8 0.8 fusion.99
  10.7 0.8 bitcast_multiply_fusion.4
  13.5 1.0 convolution_bitcast_fusion.7
  19.8 0.6 convolution_bitcast_fusion
  20.4 0.7 concatenate.64
  22.2 1.0 fusion.116
  23.4 0.8 copy.398
  24.6 1.8 reshape.326
  26.6 0.8 dynamic_slice.3
  27.7 0.6 fusion.75
  28.3 2.5 fusion.48
  30.8 5.7 %fusion.108 = f32[256,4,2048]{2,0,1:T(8,128)} fusion(s32[256]{0:T(256)S(1)} %dynamic_slice.3, f32[4,1,2048,4]{2,1,3,0:T(1,128)S(1)} %fusion.116), kind=kOutput, calls=%fused_computation.187 | convolution fusion | flops 100664320 | bytes 8520704 | tf_op jit(solution)/shard_map/rk,kcj->rcj/dot_general | solution.py:156
  36.6 210.1 %all-gather.2.cloned.1.call-done = bf16[8192,2048]{1,0:T(8,128)(2,1)} async-done(((bf16[256,2048]{1,0:T(8,128)(2,1)}), bf16[8192,2048]{1,0:T(8,128)(2,1)}) %all-gather.2.cloned.1.call-update) | async-done | bytes 33554448 | tf_op jit(solution)/shard_map/all_gather | solution.py:117
  246.7 16.6 %conditional.1 = (bf16[256,256]{1,0:T(8,128)(2,1)S(1)}, bf16[256,256]{1,0:T(8,128)(2,1)S(1)}, bf16[256,256]{1,0:T(8,128)(2,1)S(1)}, bf16[256,256]{1,0:T(8,128)(2...) conditional(s32[]{:T(128)} %convert_element_type.36, () %tuple.23, ...), branch_computations={%region_0.0_spmd, %region_1.0_spmd} | conditional | flops 8590458880 | bytes 40894528 | solution.py:104
  246.7 16.5 %convolution_convert_fusion = bf16[256,2048]{1,0:T(8,128)(2,1)S(1)} fusion(bf16[256,8192]{1,0:T(8,128)(2,1)} %get-tuple-element.79, bf16[8192,2048]{1,0:T(8,128)(2,1)} %get-tuple-element.54), kind=kOutput, calls=%fused_computation | convolution fusion | flops 8590458880 | bytes 38797312 | tf_op jit(solution)/shard_map/cond/branch_1_fun/dot_general | solution.py:99
  263.6 1.0 fusion.3
  264.7 1.0 fusion.4
  265.9 1.0 fusion.5
  270.6 0.8 copy.313
  271.4 0.8 copy.306
  272.2 35.0 %while.10 = (s32[]{:T(128)}, f32[4,256]{1,0:T(4,128)S(1)}, f32[4,4,256]{2,1,0:T(4,128)S(1)}, f32[4,256]{1,0:T(4,128)S(1)}, s32[]{:T(128)}) while((s32[]{:T(128)}, f32[4,256]{1,0:T(4,128)S(1)}, f32[4,4,256]{2,1,0:T(4,128)S(1)}, f32[4,256]{1,0:T(4,128)S(1)}, s32[]{:T(128)}) %tuple.57), condition=%wide.region_19.0_spmd, body=%wide.region_18.0_spmd.sunk | while | flops 8194 | bytes 53349 | solution.py:153
  272.3 4.0 %collective-permute-start = (f32[4,256]{1,0:T(4,128)S(1)}, f32[4,256]{1,0:T(4,128)S(1)}, u32[]{:S(2)}, u32[]{:S(2)}) collective-permute-start(f32[4,256]{1,0:T(4,128)S(1)} %bitcast_add_fusion.11), channel_id=1, source_target_pairs={{0,1},{1,2},{2,3},{3,4},{4,5},{5,6},{6,7},{8,9},{9,10},{10,11},{11... | collective-permute-start | bytes 12296 | tf_op jit(solution)/shard_map/while/body/eval_jaxpr/ppermute | solution.py:15
  276.3 0.7 collective-permute-done
  277.1 4.2 %collective-permute-start = (f32[4,256]{1,0:T(4,128)S(1)}, f32[4,256]{1,0:T(4,128)S(1)}, u32[]{:S(2)}, u32[]{:S(2)}) collective-permute-start(f32[4,256]{1,0:T(4,128)S(1)} %bitcast_add_fusion.11), channel_id=1, source_target_pairs={{0,1},{1,2},{2,3},{3,4},{4,5},{5,6},{6,7},{8,9},{9,10},{10,11},{11... | collective-permute-start | bytes 12296 | tf_op jit(solution)/shard_map/while/body/eval_jaxpr/ppermute | solution.py:15
  281.3 0.7 collective-permute-done
  282.0 4.2 %collective-permute-start = (f32[4,256]{1,0:T(4,128)S(1)}, f32[4,256]{1,0:T(4,128)S(1)}, u32[]{:S(2)}, u32[]{:S(2)}) collective-permute-start(f32[4,256]{1,0:T(4,128)S(1)} %bitcast_add_fusion.11), channel_id=1, source_target_pairs={{0,1},{1,2},{2,3},{3,4},{4,5},{5,6},{6,7},{8,9},{9,10},{10,11},{11... | collective-permute-start | bytes 12296 | tf_op jit(solution)/shard_map/while/body/eval_jaxpr/ppermute | solution.py:15
  286.2 0.7 collective-permute-done
  287.0 4.2 %collective-permute-start = (f32[4,256]{1,0:T(4,128)S(1)}, f32[4,256]{1,0:T(4,128)S(1)}, u32[]{:S(2)}, u32[]{:S(2)}) collective-permute-start(f32[4,256]{1,0:T(4,128)S(1)} %bitcast_add_fusion.11), channel_id=1, source_target_pairs={{0,1},{1,2},{2,3},{3,4},{4,5},{5,6},{6,7},{8,9},{9,10},{10,11},{11... | collective-permute-start | bytes 12296 | tf_op jit(solution)/shard_map/while/body/eval_jaxpr/ppermute | solution.py:15
  291.2 0.7 collective-permute-done
  292.0 4.2 %collective-permute-start = (f32[4,256]{1,0:T(4,128)S(1)}, f32[4,256]{1,0:T(4,128)S(1)}, u32[]{:S(2)}, u32[]{:S(2)}) collective-permute-start(f32[4,256]{1,0:T(4,128)S(1)} %bitcast_add_fusion.11), channel_id=1, source_target_pairs={{0,1},{1,2},{2,3},{3,4},{4,5},{5,6},{6,7},{8,9},{9,10},{10,11},{11... | collective-permute-start | bytes 12296 | tf_op jit(solution)/shard_map/while/body/eval_jaxpr/ppermute | solution.py:15
  296.2 0.7 collective-permute-done
  296.9 4.2 %collective-permute-start = (f32[4,256]{1,0:T(4,128)S(1)}, f32[4,256]{1,0:T(4,128)S(1)}, u32[]{:S(2)}, u32[]{:S(2)}) collective-permute-start(f32[4,256]{1,0:T(4,128)S(1)} %bitcast_add_fusion.11), channel_id=1, source_target_pairs={{0,1},{1,2},{2,3},{3,4},{4,5},{5,6},{6,7},{8,9},{9,10},{10,11},{11... | collective-permute-start | bytes 12296 | tf_op jit(solution)/shard_map/while/body/eval_jaxpr/ppermute | solution.py:15
  301.1 0.7 collective-permute-done
  301.9 4.2 %collective-permute-start = (f32[4,256]{1,0:T(4,128)S(1)}, f32[4,256]{1,0:T(4,128)S(1)}, u32[]{:S(2)}, u32[]{:S(2)}) collective-permute-start(f32[4,256]{1,0:T(4,128)S(1)} %bitcast_add_fusion.11), channel_id=1, source_target_pairs={{0,1},{1,2},{2,3},{3,4},{4,5},{5,6},{6,7},{8,9},{9,10},{10,11},{11... | collective-permute-start | bytes 12296 | tf_op jit(solution)/shard_map/while/body/eval_jaxpr/ppermute | solution.py:15
  306.1 0.7 collective-permute-done
  307.4 3.4 fusion.46
  310.8 3.4 fusion.44
  314.3 2.5 fusion.42
  316.8 2.5 fusion.40
  319.4 2.7 fusion.38
  322.1 2.5 fusion.36
  324.7 2.5 fusion.34
  327.3 23.8 %fusion = f32[256,1,2048]{2,1,0:T(1,128)S(1)} fusion(f32[4,256,1]{0,2,1:T(1,128)S(1)} %copy.356, f32[256,4,2048]{2,0,1:T(8,128)} %fusion.108), kind=kOutput, calls=%fused_computation.3 | convolution fusion | flops 25165824 | bytes 10489856 | tf_op jit(solution)/shard_map/rcj,cr->rj/dot_general | solution.py:157
  351.4 2.4 bitcast_add_fusion.1
  (137 shorter events, 14.5 us)
Async XLA Ops:
  6.5 240.1 %all-gather.2.cloned.1.call-start = ((), (), s32[]{:S(2)}) async-start(), calls=%async_computation | async-start | bytes 34603008 | tf_op jit(solution)/shard_map/all_gather | solution.py:117
  272.3 4.8 %collective-permute-start = (f32[4,256]{1,0:T(4,128)S(1)}, f32[4,256]{1,0:T(4,128)S(1)}, u32[]{:S(2)}, u32[]{:S(2)}) collective-permute-start(f32[4,256]{1,0:T(4,128)S(1)} %bitcast_add_fusion.11), channel_id=1, source_target_pairs={{0,1},{1,2},{2,3},{3,4},{4,5},{5,6},{6,7},{8,9},{9,10},{10,11},{11... | collective-permute-start | bytes 12296 | tf_op jit(solution)/shard_map/while/body/eval_jaxpr/ppermute | solution.py:15
  277.1 4.9 %collective-permute-start = (f32[4,256]{1,0:T(4,128)S(1)}, f32[4,256]{1,0:T(4,128)S(1)}, u32[]{:S(2)}, u32[]{:S(2)}) collective-permute-start(f32[4,256]{1,0:T(4,128)S(1)} %bitcast_add_fusion.11), channel_id=1, source_target_pairs={{0,1},{1,2},{2,3},{3,4},{4,5},{5,6},{6,7},{8,9},{9,10},{10,11},{11... | collective-permute-start | bytes 12296 | tf_op jit(solution)/shard_map/while/body/eval_jaxpr/ppermute | solution.py:15
  282.0 4.9 %collective-permute-start = (f32[4,256]{1,0:T(4,128)S(1)}, f32[4,256]{1,0:T(4,128)S(1)}, u32[]{:S(2)}, u32[]{:S(2)}) collective-permute-start(f32[4,256]{1,0:T(4,128)S(1)} %bitcast_add_fusion.11), channel_id=1, source_target_pairs={{0,1},{1,2},{2,3},{3,4},{4,5},{5,6},{6,7},{8,9},{9,10},{10,11},{11... | collective-permute-start | bytes 12296 | tf_op jit(solution)/shard_map/while/body/eval_jaxpr/ppermute | solution.py:15
  287.0 4.9 %collective-permute-start = (f32[4,256]{1,0:T(4,128)S(1)}, f32[4,256]{1,0:T(4,128)S(1)}, u32[]{:S(2)}, u32[]{:S(2)}) collective-permute-start(f32[4,256]{1,0:T(4,128)S(1)} %bitcast_add_fusion.11), channel_id=1, source_target_pairs={{0,1},{1,2},{2,3},{3,4},{4,5},{5,6},{6,7},{8,9},{9,10},{10,11},{11... | collective-permute-start | bytes 12296 | tf_op jit(solution)/shard_map/while/body/eval_jaxpr/ppermute | solution.py:15
  292.0 4.9 %collective-permute-start = (f32[4,256]{1,0:T(4,128)S(1)}, f32[4,256]{1,0:T(4,128)S(1)}, u32[]{:S(2)}, u32[]{:S(2)}) collective-permute-start(f32[4,256]{1,0:T(4,128)S(1)} %bitcast_add_fusion.11), channel_id=1, source_target_pairs={{0,1},{1,2},{2,3},{3,4},{4,5},{5,6},{6,7},{8,9},{9,10},{10,11},{11... | collective-permute-start | bytes 12296 | tf_op jit(solution)/shard_map/while/body/eval_jaxpr/ppermute | solution.py:15
  296.9 4.9 %collective-permute-start = (f32[4,256]{1,0:T(4,128)S(1)}, f32[4,256]{1,0:T(4,128)S(1)}, u32[]{:S(2)}, u32[]{:S(2)}) collective-permute-start(f32[4,256]{1,0:T(4,128)S(1)} %bitcast_add_fusion.11), channel_id=1, source_target_pairs={{0,1},{1,2},{2,3},{3,4},{4,5},{5,6},{6,7},{8,9},{9,10},{10,11},{11... | collective-permute-start | bytes 12296 | tf_op jit(solution)/shard_map/while/body/eval_jaxpr/ppermute | solution.py:15
  301.9 4.9 %collective-permute-start = (f32[4,256]{1,0:T(4,128)S(1)}, f32[4,256]{1,0:T(4,128)S(1)}, u32[]{:S(2)}, u32[]{:S(2)}) collective-permute-start(f32[4,256]{1,0:T(4,128)S(1)} %bitcast_add_fusion.11), channel_id=1, source_target_pairs={{0,1},{1,2},{2,3},{3,4},{4,5},{5,6},{6,7},{8,9},{9,10},{10,11},{11... | collective-permute-start | bytes 12296 | tf_op jit(solution)/shard_map/while/body/eval_jaxpr/ppermute | solution.py:15
  327.2 23.8 %copy-start.2 = (f32[256,256]{1,0:T(8,128)S(1)}, f32[256,256]{1,0:T(8,128)}, u32[]{:S(2)}) copy-start(f32[256,256]{1,0:T(8,128)} %fusion.3) | copy-start | bytes 786436
  327.3 23.9 %copy-start.1 = (f32[256,256]{1,0:T(8,128)S(1)}, f32[256,256]{1,0:T(8,128)}, u32[]{:S(2)}) copy-start(f32[256,256]{1,0:T(8,128)} %fusion.4) | copy-start | bytes 786436
  327.3 23.9 %copy-start = (f32[256,256]{1,0:T(8,128)S(1)}, f32[256,256]{1,0:T(8,128)}, u32[]{:S(2)}) copy-start(f32[256,256]{1,0:T(8,128)} %fusion.5) | copy-start | bytes 786436
Sparse Core Ops, SparseCore 0:
  10.0 236.6 all-gather.1
where the time goes:
time: 365 us; the launch traced here: 361 us
  waiting for transfers between devices  216 us (59%)
  matrix products  80.2 us (22%)
  starting transfers between devices  29.2 us (8%)
  between operations  14.3 us (4%)
  local copies, waits for them, and re-layouts  13.5 us (4%)
  other arithmetic  7.22 us (2%)
    all_gather x1, waiting for transfers between devices, body(): lax.all_gather(white_noise, 'sup', axis=0, tiled=True)  210 us
    ppermute x7, starting transfers between devices, passed_along(): return lax.ppermute(value, axis, pairs)  29.2 us
    dot_general x1, matrix products, body(): jnp.einsum('rcj,cr->rj', gain_block, incoming, precision=PRECISE)  23.8 us
    dot_general x8, matrix products, filter_group(): jnp.einsum('rcj,cr->rj', gain_rows, carry_state, precision=PRECISE)  22.2 us
    dot_general x1, matrix products, product(): return jnp.dot(left_rows, piece_rows, preferred_element_type=jnp.float32)  16.5 us
  transfers between devices with their start and end apart: 8, of which 8 were waited for; matrix products, arithmetic and copies ran while one was open for 8% of the time, Pallas kernels for 0%

commit v1 on v0

v1 whole, which is shorter than its diff:
```python
import functools

import jax
import jax.numpy as jnp
from jax import lax
from jax.experimental import pallas as pl
from jax.experimental.pallas import tpu as pltpu
from jax.sharding import Mesh, PartitionSpec as P

CH = 256
NX, NZ, NY, NCORE = 4, 8, 4, 2
ROWS = 256
SLAB = 512
QUARTER = 2048
PACK = 80
F32 = jnp.float32
BF16 = jnp.bfloat16
PRECISE = lax.Precision.HIGHEST


def system(site_decay, site_angle, site_mix):
    radius = 1.0 - site_decay
    norm_gain = jnp.sqrt(site_decay * (2.0 - site_decay))
    cos_ground = radius[0] * jnp.cos(site_angle[0])
    sin_ground = radius[0] * jnp.sin(site_angle[0])
    cos_high = radius[1] * jnp.cos(site_angle[1])
    sin_high = radius[1] * jnp.sin(site_angle[1])
    zeros_row = jnp.zeros_like(cos_ground)
    ones_row = jnp.ones_like(cos_ground)
    mix_a, mix_b, out_a, out_b = (site_mix[0], site_mix[1], site_mix[2], site_mix[3])
    row_list = [
        [cos_ground, -sin_ground, zeros_row, zeros_row],
        [sin_ground, cos_ground, zeros_row, zeros_row],
        [
            norm_gain[0] * (mix_a * cos_ground + mix_b * sin_ground),
            norm_gain[0] * (mix_b * cos_ground - mix_a * sin_ground),
            cos_high,
            -sin_high,
        ],
        [zeros_row, zeros_row, sin_high, cos_high],
    ]
    matrix = jnp.stack([jnp.stack(entries, axis=-1) for entries in row_list], axis=1)
    entry_vec = jnp.stack([ones_row, zeros_row, norm_gain[0] * mix_a, zeros_row], axis=-1)
    readout = jnp.stack([zeros_row, zeros_row, norm_gain[1] * out_a, norm_gain[1] * out_b], axis=-1)
    return (matrix, entry_vec, readout)


def tables(site_decay, site_angle, site_mix):
    matrix, entry_vec, readout = system(site_decay, site_angle, site_mix)
    classes = matrix.shape[0]
    powers = matrix[None]
    while powers.shape[0] < CH:
        further = jnp.einsum("kab,jkbc->jkac", powers[-1], powers, precision=PRECISE)
        powers = jnp.concatenate([powers, further], axis=0)
    gains = jnp.einsum("ka,jkab->kbj", readout, powers, precision=PRECISE)
    responses = jnp.einsum("jkab,kb->kja", powers[: CH - 1], entry_vec, precision=PRECISE)
    responses = jnp.concatenate([entry_vec[:, None, :], responses], axis=1)
    impulse = jnp.einsum("ka,kma->km", readout, responses, precision=PRECISE)
    padded_len = 2 * CH
    padded = jnp.concatenate([impulse, jnp.zeros((classes, CH), F32)], axis=1)
    tiled = jnp.tile(padded, (1, CH))[:, : CH * (padded_len - 1)]
    toeplitz = tiled.reshape(classes, CH, padded_len - 1)[:, :, :CH]
    toeplitz = toeplitz.reshape(classes * CH, CH).astype(BF16)
    final = responses[:, ::-1, :].transpose(0, 2, 1).astype(BF16)
    final = jnp.concatenate([final, jnp.zeros_like(final)], axis=1).reshape(classes * 8, CH)
    gains = gains.reshape(classes * 4, CH)
    gains_hi = gains.astype(BF16)
    gains_lo = (gains - gains_hi.astype(F32)).astype(BF16)
    gain_stack = jnp.concatenate([gains_hi, gains_lo, gains_hi], axis=0)
    power = powers[-1]
    power_two = jnp.einsum("kab,kbc->kac", power, power, precision=PRECISE)
    return toeplitz, final, gain_stack, power, power_two


def per_row(power, onehot):
    return jnp.sum(power.transpose(2, 1, 0)[:, :, :, None] * onehot[None, None], axis=2)


def apply_power(table, state):
    out = table[0] * state[0:1]
    for b in range(1, 4):
        out = out + table[b] * state[b : b + 1]
    return out


def factor_block(g_ref, s):
    parts = [g_ref[s, :, 0:32, :]]
    if s >= 1:
        parts.append(g_ref[s, :, 32:64, :])
    if s >= 2:
        low = g_ref[1, :, 64:80, :] if s == 2 else g_ref[0, :, 32:48, :]
        parts.append(jnp.concatenate([g_ref[s, :, 64:80, :], low], axis=1))
    if s >= 3:
        parts.append(g_ref[0, :, 48:80, :])
    return jnp.concatenate([p.reshape(ROWS, CH) for p in parts], axis=1)


def product_kernel(blocks, has_acc, last, *refs):
    refs = list(refs)
    refs.pop(0)
    acc_ref = refs.pop(0) if has_acc else None
    g_refs = [refs.pop(0) for _ in range(blocks)]
    n_refs = [refs.pop(0) for _ in range(blocks)] if not last else [refs.pop(0), refs.pop(0)]
    if last:
        final_ref, onehot_ref, out_ref, end_ref = refs
    else:
        (out_ref,) = refs
    for s in range(NX):
        rows = pl.ds(s * ROWS, ROWS)
        depth = (s + 1) * ROWS
        total = acc_ref[rows, :] if has_acc else None
        for b in range(blocks):
            if last:
                noise = n_refs[0][0 : min(depth, 512), :]
                if depth > 512:
                    noise = jnp.concatenate([noise, n_refs[1][0 : depth - 512, :]], axis=0)
            else:
                noise = n_refs[b][0:depth, :]
            term = jnp.dot(factor_block(g_refs[b], s), noise, preferred_element_type=F32)
            total = term if total is None else total + term
        if last:
            out_ref[rows, :] = total.astype(BF16)
        else:
            out_ref[rows, :] = total
    if last:
        ends = lax.dot_general(
            final_ref[...], out_ref[...], (((1,), (1,)), ((), ())), preferred_element_type=F32
        )
        picked = onehot_ref[0:1, :] * ends[0:8]
        for k in range(1, 4):
            picked = picked + onehot_ref[k : k + 1, :] * ends[k * 8 : k * 8 + 8]
        end_ref[...] = picked


def product(acc, gathered, where_z, noise_blocks, last=None):
    blocks = len(where_z)
    width = noise_blocks[0].shape[1]
    scalars = jnp.stack(where_z).astype(jnp.int32)

    def g_spec(b):
        return pl.BlockSpec((NX, 8, PACK, CH), lambda i, zs: (0, 0, 0, zs[b]))

    def whole(shape):
        return pl.BlockSpec(shape, lambda i, zs: (0,) * len(shape))

    args, specs = [], []
    if acc is not None:
        args.append(acc)
        specs.append(whole(acc.shape))
    args += [gathered] * blocks
    specs += [g_spec(b) for b in range(blocks)]
    args += noise_blocks
    specs += [whole(n.shape) for n in noise_blocks]
    rows = NX * ROWS
    if last is None:
        out_shape = jax.ShapeDtypeStruct((rows, width), F32)
        out_specs = whole((rows, width))
    else:
        args += list(last)
        specs += [whole(a.shape) for a in last]
        out_shape = (
            jax.ShapeDtypeStruct((rows, width), BF16),
            jax.ShapeDtypeStruct((8, rows), F32),
        )
        out_specs = (whole((rows, width)), whole((8, rows)))
    return pl.pallas_call(
        functools.partial(product_kernel, blocks, acc is not None, last is not None),
        grid_spec=pltpu.PrefetchScalarGridSpec(
            num_scalar_prefetch=1, grid=(1,), in_specs=specs, out_specs=out_specs
        ),
        out_shape=out_shape,
        compiler_params=pltpu.CompilerParams(vmem_limit_bytes=40 * 1024 * 1024),
        cost_estimate=pl.CostEstimate(
            flops=blocks * 2 * 10 * ROWS * CH * width,
            bytes_accessed=blocks * (1310720 + 524288) + 2097152,
            transcendentals=0,
        ),
    )(scalars, *args)


def filter_kernel(
    place, first_ref, second_ref, slabs_ref, mask_ref, onehot_ref, one_ref, two_ref,
    toeplitz_ref, final_ref, gain_ref, out_ref, state_ref,
):
    step = pl.program_id(0)
    one = [one_ref[b] for b in range(4)]

    @pl.when(step == 0)
    def _():
        two = [two_ref[b] for b in range(4)]

        def advance(t, state):
            return apply_power(two, state) + slabs_ref[t]

        state_ref[...] = lax.fori_loop(0, place[0], advance, jnp.zeros((4, ROWS), F32))

    state = state_ref[...]
    for half, ref in enumerate((first_ref, second_ref)):
        local = ref[0]
        masked = jnp.concatenate([local * mask_ref[:, k : k + 1] for k in range(4)], axis=1)
        spread = jnp.concatenate([onehot_ref[k : k + 1, :] * state for k in range(4)], axis=0)
        high = spread.astype(BF16)
        low = (spread - high.astype(F32)).astype(BF16)
        stacked = jnp.concatenate([high, high, low], axis=0)
        carried = lax.dot_general(
            stacked, gain_ref[...], (((0,), (0,)), ((), ())), preferred_element_type=F32
        )
        out_ref[:, half * CH : (half + 1) * CH] = (
            jnp.dot(masked, toeplitz_ref[...], preferred_element_type=F32) + carried
        )
        ends = lax.dot_general(
            final_ref[...], local, (((1,), (1,)), ((), ())), preferred_element_type=F32
        )
        entered = onehot_ref[0:1, :] * ends[0:4]
        for k in range(1, 4):
            entered = entered + onehot_ref[k : k + 1, :] * ends[k * 8 : k * 8 + 4]
        state = apply_power(one, state) + entered
    state_ref[...] = state


def filtered(place, first, second, slabs, mask, onehot, one, two, toeplitz, final, gain):
    def whole(a):
        return pl.BlockSpec(a.shape, lambda i, zs: (0,) * a.ndim)

    piece = pl.BlockSpec((1, ROWS, CH), lambda i, zs: (i, 0, 0))
    rest = (slabs, mask, onehot, one, two, toeplitz, final, gain)
    return pl.pallas_call(
        filter_kernel,
        grid_spec=pltpu.PrefetchScalarGridSpec(
            num_scalar_prefetch=1,
            grid=(NX,),
            in_specs=[piece, piece] + [whole(a) for a in rest],
            out_specs=pl.BlockSpec((ROWS, SLAB), lambda i, zs: (0, i)),
            scratch_shapes=[pltpu.VMEM((4, ROWS), F32)],
        ),
        out_shape=jax.ShapeDtypeStruct((ROWS, NX * SLAB), F32),
        compiler_params=pltpu.CompilerParams(vmem_limit_bytes=40 * 1024 * 1024),
        cost_estimate=pl.CostEstimate(
            flops=8 * 2 * ROWS * CH * 1100, bytes_accessed=4 * 1024 * 1024, transcendentals=0
        ),
    )(place, first, second, *rest)


def ring(value, by):
    return lax.ppermute(value, "z", [(i, (i + by) % NZ) for i in range(NZ)])


def body(factor, white_noise, site_class, site_decay, site_angle, site_mix):
    x = lax.axis_index("x")
    z = lax.axis_index("z")
    tm = lax.axis_index("y") * NCORE + lax.axis_index("c")

    mine = lax.dynamic_slice(factor, (tm * 32, 0), (32, factor.shape[1]))
    quarter = [mine[:, q * QUARTER : (q + 1) * QUARTER] for q in range(4)]
    surplus = jnp.concatenate([quarter[2][16:], quarter[3]], axis=0)
    taken = lax.ppermute(surplus, "x", [(3, 0), (2, 1)])
    share = jnp.concatenate(
        [
            quarter[0],
            jnp.where(x == 0, taken[:32], quarter[1]),
            jnp.where(x == 0, taken[32:48], jnp.where(x == 1, taken[:16], quarter[2][:16])),
        ],
        axis=0,
    )
    gathered = lax.all_gather(share, ("x", "y", "c"))
    gathered = gathered.reshape(NX, 8, PACK, QUARTER)

    toeplitz, final, gain, power, power_two = tables(site_decay, site_angle, site_mix)
    by_block = site_class.reshape(NX, NZ, ROWS)
    ids = jnp.arange(4, dtype=jnp.int32)
    tile_class = lax.dynamic_slice(by_block, (0, z, 0), (NX, 1, ROWS)).reshape(1, NX * ROWS)
    tile_hot = (tile_class == ids[:, None]).astype(F32)
    own_class = lax.dynamic_slice(by_block, (x, z, 0), (1, 1, ROWS)).reshape(1, ROWS)
    own_hot = (own_class == ids[:, None]).astype(F32)
    own_mask = (own_class.reshape(ROWS, 1) == ids[None, :]).astype(BF16)

    cut = white_noise.reshape(ROWS, NX, 2, CH)
    excitation, ends = [], []
    for half in range(2):
        slabs = cut[:, :, half, :].transpose(1, 0, 2).reshape(NX * ROWS, CH)
        own = lax.all_to_all(slabs, "x", 0, 0, tiled=True)
        up1, down1 = ring(own, 1), ring(own, -1)
        up2, down2 = ring(up1, 1), ring(down1, -1)
        up3, down3 = ring(up2, 1), ring(down2, -1)
        up4, down4 = ring(up3[:512], 1), ring(down3[512:], -1)
        total = product(None, gathered, [z, (z + 7) % 8, (z + 1) % 8], [own, up1, down1])
        total = product(total, gathered, [(z + 6) % 8, (z + 2) % 8], [up2, down2])
        total = product(total, gathered, [(z + 5) % 8, (z + 3) % 8], [up3, down3])
        local, end = product(total, gathered, [(z + 4) % 8], [up4, down4], (final, tile_hot))
        ends.append(end[:4])
        excitation.append(
            lax.all_to_all(local, "x", 0, 0, tiled=True).reshape(NX, ROWS, CH)
        )
    slab_end = apply_power(per_row(power, tile_hot), ends[0]) + ends[1]
    all_ends = lax.all_gather(slab_end, ("y", "c", "x"))
    own_ends = lax.dynamic_slice(all_ends, (0, 0, x * ROWS), (32, 4, ROWS))
    return filtered(
        jnp.reshape(tm * NX, (1,)).astype(jnp.int32),
        excitation[0], excitation[1], own_ends, own_mask, own_hot,
        per_row(power, own_hot), per_row(power_two, own_hot), toeplitz, final, gain,
    )


def solution(mesh):
    fine = Mesh(mesh.devices.reshape(NX, NZ, NY, NCORE), ("x", "z", "y", "c"))
    rows = ("x", "z")
    in_specs = (P(rows, None), P(rows, ("y", "c")), P(), P(), P(), P())
    return jax.shard_map(
        body, mesh=fine, in_specs=in_specs, out_specs=P(rows, ("y", "c")), check_vma=False
    )
```

time: 365 us -> 237 us (0.65)
  waiting for transfers between devices: 216 us -> 37.8 us
  matrix products: 80.2 us -> 6.12 us
  blocking collectives: 0 us -> 50 us
  local copies, waits for them, and re-layouts: 13.5 us -> 50.3 us
  Pallas kernels: 0 us -> 24.1 us
  starting transfers between devices: 29.2 us -> 47.3 us
    all_gather x1, waiting for transfers between devices: 210 us -> 0.01 us  [body(): gathered = lax.all_gather(share, ('x', 'y', 'c'))]
    dot_general x41 -> x9, matrix products: 79 us -> 2.53 us  [the longest x8 2.37 us: tables(): jnp.einsum('kab,jkbc->jkac', powers[-1], powers, precision=PRECISE)]
    all_gather x0 -> x1, blocking collectives: none -> 50 us  [body(): all_ends = lax.all_gather(slab_end, ('y', 'c', 'x'))]
    ppermute x7 -> x17, waiting for transfers between devices: 5.1 us -> 37.8 us  [the longest x16 31.5 us: ring(): return lax.ppermute(value, 'z', [(i, (i + by) % NZ) for i in range(NZ)])]
    unnamed x9 -> x63, local copies, waits for them, and re-layouts: 1 us -> 27.7 us
    pallas_call x0 -> x9, Pallas kernels: none -> 24.1 us  [the longest x8 20.2 us: product(): pl.pallas_call(functools.partial(product_kernel, blocks, acc is not None,...]
    all_to_all x0 -> x4, starting transfers between devices: none -> 16 us  [the longest x2 8.21 us: body(): lax.all_to_all(local, 'x', 0, 0, tiled=True).reshape(NX, ROWS, CH)]
    slice x17 -> x20, local copies, waits for them, and re-layouts: 2.49 us -> 12.7 us  [the longest x4 3.98 us: body(): up4, down4 = (ring(up3[:512], 1), ring(down3[512:], -1))]
  transfers between devices with their start and end apart: 8 -> 22, of which waited for: 8 -> 6; matrix products, arithmetic and copies ran while one was open for 8% -> 16% of each run, Pallas kernels for 0% -> 9%
where the time goes in v1:
time: 237 us; the launch traced here: 236 us
  local copies, waits for them, and re-layouts  50.3 us (21%)
  blocking collectives  50 us (21%)
  starting transfers between devices  47.3 us (20%)
  waiting for transfers between devices  37.8 us (16%)
  Pallas kernels  24.1 us (10%)
  between operations  14 us (6%)
  other arithmetic  6.16 us (3%)
  matrix products  6.12 us (3%)
    all_gather x1, blocking collectives, body(): all_ends = lax.all_gather(slab_end, ('y', 'c', 'x'))  50 us
    ppermute x16, waiting for transfers between devices, ring(): return lax.ppermute(value, 'z', [(i, (i + by) % NZ) for i in range(NZ)])  31.5 us
    ppermute x16, starting transfers between devices, ring(): return lax.ppermute(value, 'z', [(i, (i + by) % NZ) for i in range(NZ)])  30 us
    unnamed x63, local copies, waits for them, and re-layouts  27.7 us
    pallas_call x8, Pallas kernels, product(): pl.pallas_call(functools.partial(product_kernel, blocks, acc is not None,...  20.2 us
    all_to_all x2, starting transfers between devices, body(): lax.all_to_all(local, 'x', 0, 0, tiled=True).reshape(NX, ROWS, CH)  8.21 us
    all_to_all x2, starting transfers between devices, body(): own = lax.all_to_all(slabs, 'x', 0, 0, tiled=True)  7.8 us
    ppermute x1, waiting for transfers between devices, body(): taken = lax.ppermute(surplus, 'x', [(3, 0), (2, 1)])  6.33 us
  transfers between devices with their start and end apart: 22, of which 6 were waited for; matrix products, arithmetic and copies ran while one was open for 16% of the time, Pallas kernels for 9%

profile of v1, /device:TPU:1, one launch (start us, length us, event | category | flops | bytes accessed | tf_op | source)
XLA Modules:
  0.0 235.8 jit_solution(14390185641716792310)
XLA Ops:
  8.3 1.3 collective-permute-start
  9.6 6.3 %collective-permute-done = bf16[48,2048]{1,0:T(8,128)(2,1)S(1)} collective-permute-done((bf16[48,2048]{1,0:T(8,128)(2,1)S(1)}, bf16[48,2048]{1,0:T(8,128)(2,1)S(1)}, u32[]{:S(2)}, u32[]{:S(2)}) %collective-permute-start) | collective-permute-done | bytes 196640 | tf_op jit(solution)/shard_map/ppermute | solution.py:256
  18.7 1.8 reshape.361
  20.5 2.3 fusion.45
  23.8 3.6 %all-to-all-start = ((bf16[4,256,256]{2,1,0:T(8,128)(2,1)}), bf16[4,256,256]{2,1,0:T(8,128)(2,1)S(1)}, u32[]{:S(2)}, u32[]{:S(2)}) async-start(bf16[4,256,256]{2,1,0:T(8,128)(2,1)} %bitcast.225), calls=%async_computation | async-start | bytes 1048576 | tf_op jit(solution)/shard_map/all_to_all | solution.py:281
  34.4 3.4 %fusion.48 = f32[4,1,256,4]{1,2,3,0:T(8,128)S(1)} fusion(f32[256,4,4,4]{0,2,3,1:T(4,128)S(1)} %concatenate.58, f32[4,4,1,1]{1,2,3,0:T(1,128)S(1)} %bitcast.266), kind=kOutput, calls=%fused_computation.111 | convolution fusion | flops 196608 | bytes 81984 | tf_op jit(solution)/shard_map/ka,jkab->kbj/dot_general | solution.py:55
  38.6 2.2 copy.256
  41.0 4.2 %all-to-all-start.2 = ((bf16[4,256,256]{2,1,0:T(8,128)(2,1)}), bf16[4,256,256]{2,1,0:T(8,128)(2,1)S(1)}, u32[]{:S(2)}, u32[]{:S(2)}) async-start(bf16[4,256,256]{2,1,0:T(8,128)(2,1)} %bitcast.224), calls=%async_computation.2 | async-start | bytes 1048576 | tf_op jit(solution)/shard_map/all_to_all | solution.py:281
  46.0 3.8 %collective-permute-start.1 = (bf16[1024,256]{1,0:T(8,128)(2,1)S(1)}, bf16[1024,256]{1,0:T(8,128)(2,1)S(1)}, u32[]{:S(2)}, u32[]{:S(2)}) collective-permute-start(bf16[1024,256]{1,0:T(8,128)(2,1)S(1)} %bitcast.243), channel_id=1, source_target_pairs={{0,8},{8,16},{16,24},{24,32},{32,40},{40,48},{48,56},{56,0},{1,9},... | collective-permute-start | bytes 1572872 | tf_op jit(solution)/shard_map/ppermute | solution.py:245
  49.8 4.0 %collective-permute-start.2 = (bf16[1024,256]{1,0:T(8,128)(2,1)S(1)}, bf16[1024,256]{1,0:T(8,128)(2,1)S(1)}, u32[]{:S(2)}, u32[]{:S(2)}) collective-permute-start(bf16[1024,256]{1,0:T(8,128)(2,1)S(1)} %bitcast.244), channel_id=1, source_target_pairs={{0,56},{8,0},{16,8},{24,16},{32,24},{40,32},{48,40},{56,48},{1,57}... | collective-permute-start | bytes 1572872 | tf_op jit(solution)/shard_map/ppermute | solution.py:245
  53.8 2.3 collective-permute-start.9
  56.1 3.9 %collective-permute-start.10 = (bf16[1024,256]{1,0:T(8,128)(2,1)S(1)}, bf16[1024,256]{1,0:T(8,128)(2,1)}, u32[]{:S(2)}, u32[]{:S(2)}) collective-permute-start(bf16[1024,256]{1,0:T(8,128)(2,1)S(1)} %bitcast.247), channel_id=1, source_target_pairs={{0,56},{8,0},{16,8},{24,16},{32,24},{40,32},{48,40},{56,48},{1,57}... | collective-permute-start | bytes 1572872 | tf_op jit(solution)/shard_map/ppermute | solution.py:245
  61.0 2.8 %collective-permute-done.1.refs_5_ = bf16[1024,256]{1,0:T(8,128)(2,1)S(1)} collective-permute-done((bf16[1024,256]{1,0:T(8,128)(2,1)S(1)}, bf16[1024,256]{1,0:T(8,128)(2,1)S(1)}, u32[]{:S(2)}, u32[]{:S(2)}) %collective-permute-start.1) | collective-permute-done | bytes 524320 | tf_op jit(solution)/shard_map/ppermute | solution.py:245
  64.6 2.7 %collective-permute-start.4 = (bf16[1024,256]{1,0:T(8,128)(2,1)S(1)}, bf16[1024,256]{1,0:T(8,128)(2,1)}, u32[]{:S(2)}, u32[]{:S(2)}) collective-permute-start(bf16[1024,256]{1,0:T(8,128)(2,1)S(1)} %collective-permute-done.2.refs_6_), channel_id=1, source_target_pairs={{0,56},{8,0},{16,8},{24,16},{32,24},{40,32},{48,40},{56,48},{1,57}... | collective-permute-start | bytes 1572872 | tf_op jit(solution)/shard_map/ppermute | solution.py:245
  68.1 7.0 %collective-permute-done.9.refs_5_ = bf16[1024,256]{1,0:T(8,128)(2,1)S(1)} collective-permute-done((bf16[1024,256]{1,0:T(8,128)(2,1)S(1)}, bf16[1024,256]{1,0:T(8,128)(2,1)S(1)}, u32[]{:S(2)}, u32[]{:S(2)}) %collective-permute-start.9) | collective-permute-done | bytes 524320 | tf_op jit(solution)/shard_map/ppermute | solution.py:245
  75.9 2.7 %collective-permute-start.12 = (bf16[1024,256]{1,0:T(8,128)(2,1)}, bf16[1024,256]{1,0:T(8,128)(2,1)}, u32[]{:S(2)}, u32[]{:S(2)}) collective-permute-start(bf16[1024,256]{1,0:T(8,128)(2,1)} %collective-permute-done.10.refs_6_), channel_id=1, source_target_pairs={{0,56},{8,0},{16,8},{24,16},{32,24},{40,32},{48,40},{56,48},{1,57}... | collective-permute-start | bytes 1572872 | tf_op jit(solution)/shard_map/ppermute | solution.py:245
  78.7 7.6 %collective-permute-done.3.refs_4_ = bf16[1024,256]{1,0:T(8,128)(2,1)} collective-permute-done((bf16[1024,256]{1,0:T(8,128)(2,1)S(1)}, bf16[1024,256]{1,0:T(8,128)(2,1)}, u32[]{:S(2)}, u32[]{:S(2)}) %collective-permute-start.3) | collective-permute-done | bytes 524320 | tf_op jit(solution)/shard_map/ppermute | solution.py:245
  86.4 2.7 %collective-permute-start.6 = (bf16[1024,256]{1,0:T(8,128)(2,1)}, bf16[1024,256]{1,0:T(8,128)(2,1)S(1)}, u32[]{:S(2)}, u32[]{:S(2)}) collective-permute-start(bf16[1024,256]{1,0:T(8,128)(2,1)} %collective-permute-done.4.refs_5_), channel_id=1, source_target_pairs={{0,56},{8,0},{16,8},{24,16},{32,24},{40,32},{48,40},{56,48},{1,57}... | collective-permute-start | bytes 1572872 | tf_op jit(solution)/shard_map/ppermute | solution.py:245
  89.6 7.9 %collective-permute-done.11.refs_4_ = bf16[1024,256]{1,0:T(8,128)(2,1)S(1)} collective-permute-done((bf16[1024,256]{1,0:T(8,128)(2,1)S(1)}, bf16[1024,256]{1,0:T(8,128)(2,1)S(1)}, u32[]{:S(2)}, u32[]{:S(2)}) %collective-permute-start.11) | collective-permute-done | bytes 524320 | tf_op jit(solution)/shard_map/ppermute | solution.py:245
  97.5 2.7 %collective-permute-start.14 = (bf16[1024,256]{1,0:T(8,128)(2,1)}, bf16[1024,256]{1,0:T(8,128)(2,1)}, u32[]{:S(2)}, u32[]{:S(2)}) collective-permute-start(bf16[1024,256]{1,0:T(8,128)(2,1)} %collective-permute-done.12.refs_5_), channel_id=1, source_target_pairs={{0,56},{8,0},{16,8},{24,16},{32,24},{40,32},{48,40},{56,48},{1,57}... | collective-permute-start | bytes 1572872 | tf_op jit(solution)/shard_map/ppermute | solution.py:245
  101.6 1.1 broadcast_bitcast_fusion
  102.7 6.1 %collective-permute-done.5.refs_4_ = bf16[1024,256]{1,0:T(8,128)(2,1)S(1)} collective-permute-done((bf16[1024,256]{1,0:T(8,128)(2,1)}, bf16[1024,256]{1,0:T(8,128)(2,1)S(1)}, u32[]{:S(2)}, u32[]{:S(2)}) %collective-permute-start.5) | collective-permute-done | bytes 524320 | tf_op jit(solution)/shard_map/ppermute | solution.py:245
  110.3 2.7 %collective-permute-start.8 = (bf16[512,256]{1,0:T(8,128)(2,1)}, bf16[512,256]{1,0:T(8,128)(2,1)}, u32[]{:S(2)}, u32[]{:S(2)}) collective-permute-start(bf16[512,256]{1,0:T(8,128)(2,1)} %slice.194), channel_id=1, source_target_pairs={{0,56},{8,0},{16,8},{24,16},{32,24},{40,32},{48,40},{56,48},{1,57}... | collective-permute-start | bytes 786440 | tf_op jit(solution)/shard_map/ppermute | solution.py:245
  113.0 2.0 copy.250
  115.1 1.3 slice.210
  116.4 4.0 %reshape.364 = bf16[4,256,511]{2,1,0:T(8,128)(2,1)} reshape(bf16[4,130816]{1,0:T(4,128)(2,1)} %slice.210) | data formatting | bytes 2093056 | tf_op jit(solution)/shard_map/reshape | solution.py:62
  120.4 1.9 slice.211
  123.1 1.7 slice.204
  124.8 2.7 %collective-permute-start.16 = (bf16[512,256]{1,0:T(8,128)(2,1)}, bf16[512,256]{1,0:T(8,128)(2,1)}, u32[]{:S(2)}, u32[]{:S(2)}) collective-permute-start(bf16[512,256]{1,0:T(8,128)(2,1)} %slice.204), channel_id=1, source_target_pairs={{0,56},{8,0},{16,8},{24,16},{32,24},{40,32},{48,40},{56,48},{1,57}... | collective-permute-start | bytes 786440 | tf_op jit(solution)/shard_map/ppermute | solution.py:245
  127.4 4.0 %copy-done = bf16[2560,2048]{1,0:T(8,128)(2,1)S(1)} copy-done((bf16[2560,2048]{1,0:T(8,128)(2,1)S(1)}, bf16[2560,2048]{1,0:T(8,128)(2,1)}, u32[]{:S(2)}) %copy-start) | copy-done | bytes 10485784
  131.4 1.0 copy-done.17
  133.5 1.8 shard_map.64.refs_1_
  136.3 1.6 copy-done.1
  137.9 1.2 copy-done.5
  139.1 2.9 %shard_map.65.refs_1_ = f32[1024,256]{1,0:T(8,128)S(1)} custom-call(s32[2]{0:T(128)S(1)} %copy-done.23, f32[1024,256]{1,0:T(8,128)S(1)} %copy-done.5, bf16[4,8,80,2048]{3,2,1,0:T(8,128)(2,1)S(1)} %bitcast.230, bf16[4,8,80,2048]{3,2,1,0:T(8,128)(2,1)S(1)} %bitcast.231, bf16[1024,256]{1,0:T(8,128)(2,1)} %collective-permute-done.3.refs_4_, ...), custom_call_target="tpu_custom_call" | custom-call | flops 671088640 | bytes 5767168 | tf_op jit(solution)/shard_map/pallas_call | solution.py:166
  142.0 1.5 shard_map.66.refs_1_
  143.5 2.5 %shard_map.67 = (bf16[1024,256]{1,0:T(8,128)(2,1)}, f32[8,1024]{1,0:T(8,128)S(1)}) custom-call(s32[1]{0:T(128)} %bitcast.2.refs_0_, f32[1024,256]{1,0:T(8,128)S(1)} %shard_map.66.refs_1_, bf16[4,8,80,2048]{3,2,1,0:T(8,128)(2,1)S(1)} %bitcast.234, bf16[512,256]{1,0:T(8,128)(2,1)S(1)} %collective-permute-done.7.refs_3_, ...), custom_call_target="tpu_custom_call" | custom-call | flops 335544320 | bytes 3932160 | tf_op jit(solution)/shard_map/pallas_call | solution.py:166
  146.0 4.0 %all-to-all-start.1 = ((bf16[4,256,256]{2,1,0:T(8,128)(2,1)}), bf16[4,256,256]{2,1,0:T(8,128)(2,1)S(1)}, u32[]{:S(2)}, u32[]{:S(2)}) async-start(bf16[4,256,256]{2,1,0:T(8,128)(2,1)} %bitcast.66), calls=%async_computation.1 | async-start | bytes 1048576 | tf_op jit(solution)/shard_map/all_to_all | solution.py:292
  150.0 4.0 %copy-done.2 = bf16[2560,2048]{1,0:T(8,128)(2,1)S(1)} copy-done((bf16[2560,2048]{1,0:T(8,128)(2,1)S(1)}, bf16[2560,2048]{1,0:T(8,128)(2,1)}, u32[]{:S(2)}) %copy-start.2) | copy-done | bytes 10485784
  154.0 1.0 copy-done.15
  155.0 3.4 %shard_map.68.refs_1_ = f32[1024,256]{1,0:T(8,128)S(1)} custom-call(s32[3]{0:T(128)S(1)} %pad_add_fusion.2.refs_0_, bf16[4,8,80,2048]{3,2,1,0:T(8,128)(2,1)S(1)} %bitcast.235, bf16[4,8,80,2048]{3,2,1,0:T(8,128)(2,1)S(1)} %bitcast.236, bf16[4,8,80,2048]{3,2,1,0:T(8,128)(2,1)S(1)} %bitcast.237, bf16[1024,256]{1,0:T(8,128)(2,1)S(1)} %bitcast.248, ...), custom_call_target="tpu_custom_call" | custom-call | flops 1006632960 | bytes 7602176 | tf_op jit(solution)/shard_map/pallas_call | solution.py:166
  158.4 4.0 %copy-done.3 = bf16[2560,2048]{1,0:T(8,128)(2,1)S(1)} copy-done((bf16[2560,2048]{1,0:T(8,128)(2,1)S(1)}, bf16[2560,2048]{1,0:T(8,128)(2,1)}, u32[]{:S(2)}) %copy-start.3) | copy-done | bytes 10485784
  162.4 2.8 %shard_map.69.refs_1_ = f32[1024,256]{1,0:T(8,128)S(1)} custom-call(s32[2]{0:T(128)S(1)} %copy-done.23, f32[1024,256]{1,0:T(8,128)S(1)} %shard_map.68.refs_1_, bf16[4,8,80,2048]{3,2,1,0:T(8,128)(2,1)S(1)} %bitcast.238, bf16[4,8,80,2048]{3,2,1,0:T(8,128)(2,1)S(1)} %bitcast.239, bf16[1024,256]{1,0:T(8,128)(2,1)S(1)} %collective-permute-done.11.refs_4_, ...), custom_call_target="tpu_custom_call" | custom-call | flops 671088640 | bytes 5767168 | tf_op jit(solution)/shard_map/pallas_call | solution.py:166
  165.2 2.8 %shard_map.70.refs_1_ = f32[1024,256]{1,0:T(8,128)S(1)} custom-call(s32[2]{0:T(128)S(1)} %copy-done.22, f32[1024,256]{1,0:T(8,128)S(1)} %shard_map.69.refs_1_, bf16[4,8,80,2048]{3,2,1,0:T(8,128)(2,1)S(1)} %bitcast.240, bf16[4,8,80,2048]{3,2,1,0:T(8,128)(2,1)S(1)} %bitcast.241, bf16[1024,256]{1,0:T(8,128)(2,1)S(1)} %copy-done.13, ...), custom_call_target="tpu_custom_call" | custom-call | flops 671088640 | bytes 5767168 | tf_op jit(solution)/shard_map/pallas_call | solution.py:166
  168.1 2.6 %shard_map.71 = (bf16[1024,256]{1,0:T(8,128)(2,1)}, f32[8,1024]{1,0:T(8,128)S(1)}) custom-call(s32[1]{0:T(128)} %bitcast.2.refs_0_, f32[1024,256]{1,0:T(8,128)S(1)} %shard_map.70.refs_1_, bf16[4,8,80,2048]{3,2,1,0:T(8,128)(2,1)S(1)} %bitcast.242, bf16[512,256]{1,0:T(8,128)(2,1)} %collective-permute-done.15.refs_3_, ...), custom_call_target="tpu_custom_call" | custom-call | flops 335544320 | bytes 3932160 | tf_op jit(solution)/shard_map/pallas_call | solution.py:166
  170.7 4.2 %all-to-all-start.3 = ((bf16[4,256,256]{2,1,0:T(8,128)(2,1)}), bf16[4,256,256]{2,1,0:T(8,128)(2,1)S(1)}, u32[]{:S(2)}, u32[]{:S(2)}) async-start(bf16[4,256,256]{2,1,0:T(8,128)(2,1)} %bitcast.70), calls=%async_computation.3 | async-start | bytes 1048576 | tf_op jit(solution)/shard_map/all_to_all | solution.py:292
  175.0 50.0 %all-gather.2 = f32[32,4,1024]{2,1,0:T(4,128)S(1)} all-gather(f32[1,4,1024]{2,1,0:T(4,128)S(1)} %fusion.13), channel_id=3, replica_groups=mesh['x'=4,'z'=8,'y'=4,'c'=2] {'y','c','x'}, dimensions={0}, use_global_device_ids=true | all-gather | bytes 540672 | tf_op jit(solution)/shard_map/all_gather | solution.py:295
  225.0 3.9 %shard_map.72 = f32[256,2048]{1,0:T(8,128)} custom-call(s32[1]{0:T(128)} %bitcast.1.place, bf16[4,256,256]{2,1,0:T(8,128)(2,1)S(1)} %all-to-all-done.1.first_ref, bf16[4,256,256]{2,1,0:T(8,128)(2,1)S(1)} %all-to-all-done.3.second_ref, f32[32,4,256]{2,1,0:T(4,128)S(1)} %constant_dynamic-slice_fusion.2.slabs_ref, bf16[256,4]{1,0:T(8,128)(2,1)S(1)} %fusion.mask_ref, ...), custom_call_target="tpu_custom_call" | custom-call | flops 1153433600 | bytes 4194304 | tf_op jit(solution)/shard_map/pallas_call | solution.py:227
  (164 shorter events, 24.0 us)
Async XLA Ops:
  6.5 120.9 %all-gather.5.cloned.1.call-start = ((), (), s32[]{:S(2)}) async-start(), calls=%async_computation.4 | async-start | bytes 10813440 | tf_op jit(solution)/shard_map/all_gather | solution.py:265
  8.3 7.6 %collective-permute-start = (bf16[48,2048]{1,0:T(8,128)(2,1)S(1)}, bf16[48,2048]{1,0:T(8,128)(2,1)S(1)}, u32[]{:S(2)}, u32[]{:S(2)}) collective-permute-start(bf16[48,2048]{1,0:T(8,128)(2,1)S(1)} %pad_maximum_fusion.1), channel_id=1, source_target_pairs={{192,0},{128,64},{193,1},{129,65},{194,2},{130,66},{195,3},{131,67... | collective-permute-start | bytes 589832 | tf_op jit(solution)/shard_map/ppermute | solution.py:256
  18.6 8.7 %copy-start.28 = (f32[2,4]{1,0:T(2,128)S(1)}, f32[2,4]{1,0:T(2,128)}, u32[]{:S(2)}) copy-start(f32[2,4]{1,0:T(2,128)} %param.9) | copy-start | bytes 100
  18.6 8.8 %copy-start.26 = (f32[4,4]{1,0:T(4,128)S(1)}, f32[4,4]{1,0:T(4,128)}, u32[]{:S(2)}) copy-start(f32[4,4]{1,0:T(4,128)} %param.11) | copy-start | bytes 196
  18.7 8.7 %copy-start.27 = (f32[2,4]{1,0:T(2,128)S(1)}, f32[2,4]{1,0:T(2,128)}, u32[]{:S(2)}) copy-start(f32[2,4]{1,0:T(2,128)} %param.10) | copy-start | bytes 100
  23.8 14.9 %copy-start.25 = (s32[8192]{0:T(1024)S(1)}, s32[8192]{0:T(1024)}, u32[]{:S(2)}) copy-start(s32[8192]{0:T(1024)} %param.8) | copy-start | bytes 98308
  23.8 17.2 %all-to-all-start = ((bf16[4,256,256]{2,1,0:T(8,128)(2,1)}), bf16[4,256,256]{2,1,0:T(8,128)(2,1)S(1)}, u32[]{:S(2)}, u32[]{:S(2)}) async-start(bf16[4,256,256]{2,1,0:T(8,128)(2,1)} %bitcast.225), calls=%async_computation | async-start | bytes 1048576 | tf_op jit(solution)/shard_map/all_to_all | solution.py:281
  41.0 12.8 %all-to-all-start.2 = ((bf16[4,256,256]{2,1,0:T(8,128)(2,1)}), bf16[4,256,256]{2,1,0:T(8,128)(2,1)S(1)}, u32[]{:S(2)}, u32[]{:S(2)}) async-start(bf16[4,256,256]{2,1,0:T(8,128)(2,1)} %bitcast.224), calls=%async_computation.2 | async-start | bytes 1048576 | tf_op jit(solution)/shard_map/all_to_all | solution.py:281
  46.0 17.8 %collective-permute-start.1 = (bf16[1024,256]{1,0:T(8,128)(2,1)S(1)}, bf16[1024,256]{1,0:T(8,128)(2,1)S(1)}, u32[]{:S(2)}, u32[]{:S(2)}) collective-permute-start(bf16[1024,256]{1,0:T(8,128)(2,1)S(1)} %bitcast.243), channel_id=1, source_target_pairs={{0,8},{8,16},{16,24},{24,32},{32,40},{40,48},{48,56},{56,0},{1,9},... | collective-permute-start | bytes 1572872 | tf_op jit(solution)/shard_map/ppermute | solution.py:245
  49.8 14.9 %collective-permute-start.2 = (bf16[1024,256]{1,0:T(8,128)(2,1)S(1)}, bf16[1024,256]{1,0:T(8,128)(2,1)S(1)}, u32[]{:S(2)}, u32[]{:S(2)}) collective-permute-start(bf16[1024,256]{1,0:T(8,128)(2,1)S(1)} %bitcast.244), channel_id=1, source_target_pairs={{0,56},{8,0},{16,8},{24,16},{32,24},{40,32},{48,40},{56,48},{1,57}... | collective-permute-start | bytes 1572872 | tf_op jit(solution)/shard_map/ppermute | solution.py:245
  53.8 66.7 %copy-start.6 = (bf16[4,256,256]{2,1,0:T(8,128)(2,1)}, bf16[4,256,256]{2,1,0:T(8,128)(2,1)S(1)}, u32[]{:S(2)}) copy-start(bf16[4,256,256]{2,1,0:T(8,128)(2,1)S(1)} %all-to-all-done.2) | copy-start | bytes 1572868
  53.8 21.3 %collective-permute-start.9 = (bf16[1024,256]{1,0:T(8,128)(2,1)S(1)}, bf16[1024,256]{1,0:T(8,128)(2,1)S(1)}, u32[]{:S(2)}, u32[]{:S(2)}) collective-permute-start(bf16[1024,256]{1,0:T(8,128)(2,1)S(1)} %bitcast.246), channel_id=1, source_target_pairs={{0,8},{8,16},{16,24},{24,32},{32,40},{40,48},{48,56},{56,0},{1,9},... | collective-permute-start | bytes 1572872 | tf_op jit(solution)/shard_map/ppermute | solution.py:245
  56.1 19.9 %collective-permute-start.10 = (bf16[1024,256]{1,0:T(8,128)(2,1)S(1)}, bf16[1024,256]{1,0:T(8,128)(2,1)}, u32[]{:S(2)}, u32[]{:S(2)}) collective-permute-start(bf16[1024,256]{1,0:T(8,128)(2,1)S(1)} %bitcast.247), channel_id=1, source_target_pairs={{0,56},{8,0},{16,8},{24,16},{32,24},{40,32},{48,40},{56,48},{1,57}... | collective-permute-start | bytes 1572872 | tf_op jit(solution)/shard_map/ppermute | solution.py:245
  63.8 22.6 %collective-permute-start.3 = (bf16[1024,256]{1,0:T(8,128)(2,1)S(1)}, bf16[1024,256]{1,0:T(8,128)(2,1)}, u32[]{:S(2)}, u32[]{:S(2)}) collective-permute-start(bf16[1024,256]{1,0:T(8,128)(2,1)S(1)} %collective-permute-done.1.refs_5_), channel_id=1, source_target_pairs={{0,8},{8,16},{16,24},{24,32},{32,40},{40,48},{48,56},{56,0},{1,9},... | collective-permute-start | bytes 1572872 | tf_op jit(solution)/shard_map/ppermute | solution.py:245
  64.6 21.8 %collective-permute-start.4 = (bf16[1024,256]{1,0:T(8,128)(2,1)S(1)}, bf16[1024,256]{1,0:T(8,128)(2,1)}, u32[]{:S(2)}, u32[]{:S(2)}) collective-permute-start(bf16[1024,256]{1,0:T(8,128)(2,1)S(1)} %collective-permute-done.2.refs_6_), channel_id=1, source_target_pairs={{0,56},{8,0},{16,8},{24,16},{32,24},{40,32},{48,40},{56,48},{1,57}... | collective-permute-start | bytes 1572872 | tf_op jit(solution)/shard_map/ppermute | solution.py:245
  75.1 22.4 %collective-permute-start.11 = (bf16[1024,256]{1,0:T(8,128)(2,1)S(1)}, bf16[1024,256]{1,0:T(8,128)(2,1)S(1)}, u32[]{:S(2)}, u32[]{:S(2)}) collective-permute-start(bf16[1024,256]{1,0:T(8,128)(2,1)S(1)} %collective-permute-done.9.refs_5_), channel_id=1, source_target_pairs={{0,8},{8,16},{16,24},{24,32},{32,40},{40,48},{48,56},{56,0},{1,9},... | collective-permute-start | bytes 1572872 | tf_op jit(solution)/shard_map/ppermute | solution.py:245
  75.9 21.6 %collective-permute-start.12 = (bf16[1024,256]{1,0:T(8,128)(2,1)}, bf16[1024,256]{1,0:T(8,128)(2,1)}, u32[]{:S(2)}, u32[]{:S(2)}) collective-permute-start(bf16[1024,256]{1,0:T(8,128)(2,1)} %collective-permute-done.10.refs_6_), channel_id=1, source_target_pairs={{0,56},{8,0},{16,8},{24,16},{32,24},{40,32},{48,40},{56,48},{1,57}... | collective-permute-start | bytes 1572872 | tf_op jit(solution)/shard_map/ppermute | solution.py:245
  86.4 22.4 %collective-permute-start.5 = (bf16[1024,256]{1,0:T(8,128)(2,1)}, bf16[1024,256]{1,0:T(8,128)(2,1)S(1)}, u32[]{:S(2)}, u32[]{:S(2)}) collective-permute-start(bf16[1024,256]{1,0:T(8,128)(2,1)} %collective-permute-done.3.refs_4_), channel_id=1, source_target_pairs={{0,8},{8,16},{16,24},{24,32},{32,40},{40,48},{48,56},{56,0},{1,9},... | collective-permute-start | bytes 1572872 | tf_op jit(solution)/shard_map/ppermute | solution.py:245
  86.4 23.1 %collective-permute-start.6 = (bf16[1024,256]{1,0:T(8,128)(2,1)}, bf16[1024,256]{1,0:T(8,128)(2,1)S(1)}, u32[]{:S(2)}, u32[]{:S(2)}) collective-permute-start(bf16[1024,256]{1,0:T(8,128)(2,1)} %collective-permute-done.4.refs_5_), channel_id=1, source_target_pairs={{0,56},{8,0},{16,8},{24,16},{32,24},{40,32},{48,40},{56,48},{1,57}... | collective-permute-start | bytes 1572872 | tf_op jit(solution)/shard_map/ppermute | solution.py:245
  97.5 24.8 %collective-permute-start.13 = (bf16[1024,256]{1,0:T(8,128)(2,1)S(1)}, bf16[1024,256]{1,0:T(8,128)(2,1)S(1)}, u32[]{:S(2)}, u32[]{:S(2)}) collective-permute-start(bf16[1024,256]{1,0:T(8,128)(2,1)S(1)} %collective-permute-done.11.refs_4_), channel_id=1, source_target_pairs={{0,8},{8,16},{16,24},{24,32},{32,40},{40,48},{48,56},{56,0},{1,9},... | collective-permute-start | bytes 1572872 | tf_op jit(solution)/shard_map/ppermute | solution.py:245
  97.5 25.6 %collective-permute-start.14 = (bf16[1024,256]{1,0:T(8,128)(2,1)}, bf16[1024,256]{1,0:T(8,128)(2,1)}, u32[]{:S(2)}, u32[]{:S(2)}) collective-permute-start(bf16[1024,256]{1,0:T(8,128)(2,1)} %collective-permute-done.12.refs_5_), channel_id=1, source_target_pairs={{0,56},{8,0},{16,8},{24,16},{32,24},{40,32},{48,40},{56,48},{1,57}... | collective-permute-start | bytes 1572872 | tf_op jit(solution)/shard_map/ppermute | solution.py:245
  108.7 13.6 %copy-start.8 = (bf16[1024,256]{1,0:T(8,128)(2,1)}, bf16[1024,256]{1,0:T(8,128)(2,1)S(1)}, u32[]{:S(2)}) copy-start(bf16[1024,256]{1,0:T(8,128)(2,1)S(1)} %collective-permute-done.5.refs_4_) | copy-start | bytes 1572868
  109.5 34.0 %collective-permute-start.7 = (bf16[512,256]{1,0:T(8,128)(2,1)}, bf16[512,256]{1,0:T(8,128)(2,1)S(1)}, u32[]{:S(2)}, u32[]{:S(2)}) collective-permute-start(bf16[512,256]{1,0:T(8,128)(2,1)} %slice.193), channel_id=1, source_target_pairs={{0,8},{8,16},{16,24},{24,32},{32,40},{40,48},{48,56},{56,0},{1,9},... | collective-permute-start | bytes 786440 | tf_op jit(solution)/shard_map/ppermute | solution.py:245
  109.5 13.6 %copy-start.10 = (bf16[1024,256]{1,0:T(8,128)(2,1)}, bf16[1024,256]{1,0:T(8,128)(2,1)S(1)}, u32[]{:S(2)}) copy-start(bf16[1024,256]{1,0:T(8,128)(2,1)S(1)} %collective-permute-done.6.refs_5_) | copy-start | bytes 1572868
  110.3 33.2 %collective-permute-start.8 = (bf16[512,256]{1,0:T(8,128)(2,1)}, bf16[512,256]{1,0:T(8,128)(2,1)}, u32[]{:S(2)}, u32[]{:S(2)}) collective-permute-start(bf16[512,256]{1,0:T(8,128)(2,1)} %slice.194), channel_id=1, source_target_pairs={{0,56},{8,0},{16,8},{24,16},{32,24},{40,32},{48,40},{56,48},{1,57}... | collective-permute-start | bytes 786440 | tf_op jit(solution)/shard_map/ppermute | solution.py:245
  122.3 5.1 %copy-start.12 = (bf16[1024,256]{1,0:T(8,128)(2,1)}, bf16[1024,256]{1,0:T(8,128)(2,1)S(1)}, u32[]{:S(2)}) copy-start(bf16[1024,256]{1,0:T(8,128)(2,1)S(1)} %collective-permute-done.13.refs_4_) | copy-start | bytes 1572868
  123.1 45.0 %collective-permute-start.15 = (bf16[512,256]{1,0:T(8,128)(2,1)}, bf16[512,256]{1,0:T(8,128)(2,1)}, u32[]{:S(2)}, u32[]{:S(2)}) collective-permute-start(bf16[512,256]{1,0:T(8,128)(2,1)} %slice.203), channel_id=1, source_target_pairs={{0,8},{8,16},{16,24},{24,32},{32,40},{40,48},{48,56},{56,0},{1,9},... | collective-permute-start | bytes 786440 | tf_op jit(solution)/shard_map/ppermute | solution.py:245
  124.8 43.3 %collective-permute-start.16 = (bf16[512,256]{1,0:T(8,128)(2,1)}, bf16[512,256]{1,0:T(8,128)(2,1)}, u32[]{:S(2)}, u32[]{:S(2)}) collective-permute-start(bf16[512,256]{1,0:T(8,128)(2,1)} %slice.204), channel_id=1, source_target_pairs={{0,56},{8,0},{16,8},{24,16},{32,24},{40,32},{48,40},{56,48},{1,57}... | collective-permute-start | bytes 786440 | tf_op jit(solution)/shard_map/ppermute | solution.py:245
  127.4 4.0 %copy-start = (bf16[2560,2048]{1,0:T(8,128)(2,1)S(1)}, bf16[2560,2048]{1,0:T(8,128)(2,1)}, u32[]{:S(2)}) copy-start(bf16[2560,2048]{1,0:T(8,128)(2,1)} %all-gather.5.cloned.1.call-done) | copy-start | bytes 31457284
  131.4 1.0 copy-start.17
  132.5 1.0 copy-start.19
  133.5 4.4 %copy-start.1 = (bf16[2560,2048]{1,0:T(8,128)(2,1)S(1)}, bf16[2560,2048]{1,0:T(8,128)(2,1)}, u32[]{:S(2)}) copy-start(bf16[2560,2048]{1,0:T(8,128)(2,1)} %all-gather.5.cloned.1.call-done) | copy-start | bytes 31457284
  133.5 4.4 %copy-start.23 = (s32[2]{0:T(128)S(1)}, s32[2]{0:T(128)}, u32[]{:S(2)}) copy-start(s32[2]{0:T(128)} %pad_add_fusion.1.refs_0_) | copy-start | bytes 28
  135.3 1.0 copy-start.4
  137.9 1.2 copy-start.5
  139.1 2.9 %copy-start.9 = (bf16[1024,256]{1,0:T(8,128)(2,1)S(1)}, bf16[1024,256]{1,0:T(8,128)(2,1)}, u32[]{:S(2)}) copy-start(bf16[1024,256]{1,0:T(8,128)(2,1)} %copy-done.8) | copy-start | bytes 1572868
  139.1 2.9 %copy-start.11 = (bf16[1024,256]{1,0:T(8,128)(2,1)S(1)}, bf16[1024,256]{1,0:T(8,128)(2,1)}, u32[]{:S(2)}) copy-start(bf16[1024,256]{1,0:T(8,128)(2,1)} %copy-done.10) | copy-start | bytes 1572868
  139.1 2.9 %copy-start.22 = (s32[2]{0:T(128)S(1)}, s32[2]{0:T(128)}, u32[]{:S(2)}) copy-start(s32[2]{0:T(128)} %pad_add_fusion.refs_0_) | copy-start | bytes 28
  143.5 6.5 %copy-start.7 = (bf16[4,256,256]{2,1,0:T(8,128)(2,1)S(1)}, bf16[4,256,256]{2,1,0:T(8,128)(2,1)}, u32[]{:S(2)}) copy-start(bf16[4,256,256]{2,1,0:T(8,128)(2,1)} %copy-done.6) | copy-start | bytes 1572868
  146.0 24.7 %all-to-all-start.1 = ((bf16[4,256,256]{2,1,0:T(8,128)(2,1)}), bf16[4,256,256]{2,1,0:T(8,128)(2,1)S(1)}, u32[]{:S(2)}, u32[]{:S(2)}) async-start(bf16[4,256,256]{2,1,0:T(8,128)(2,1)} %bitcast.66), calls=%async_computation.1 | async-start | bytes 1048576 | tf_op jit(solution)/shard_map/all_to_all | solution.py:292
  150.0 4.0 %copy-start.2 = (bf16[2560,2048]{1,0:T(8,128)(2,1)S(1)}, bf16[2560,2048]{1,0:T(8,128)(2,1)}, u32[]{:S(2)}) copy-start(bf16[2560,2048]{1,0:T(8,128)(2,1)} %all-gather.5.cloned.1.call-done) | copy-start | bytes 31457284
  154.0 1.0 copy-start.15
  158.4 4.0 %copy-start.3 = (bf16[2560,2048]{1,0:T(8,128)(2,1)S(1)}, bf16[2560,2048]{1,0:T(8,128)(2,1)}, u32[]{:S(2)}) copy-start(bf16[2560,2048]{1,0:T(8,128)(2,1)} %all-gather.5.cloned.1.call-done) | copy-start | bytes 31457284
  162.4 2.8 %copy-start.13 = (bf16[1024,256]{1,0:T(8,128)(2,1)S(1)}, bf16[1024,256]{1,0:T(8,128)(2,1)}, u32[]{:S(2)}) copy-start(bf16[1024,256]{1,0:T(8,128)(2,1)} %copy-done.12) | copy-start | bytes 1572868
  168.0 6.9 %copy-start.24 = (f32[4,4,1024]{2,1,0:T(4,128)S(1)}, f32[4,4,1024]{2,1,0:T(4,128)}, u32[]{:S(2)}) copy-start(f32[4,4,1024]{2,1,0:T(4,128)} %multiply_reduce_fusion) | copy-start | bytes 196612
  168.0 57.0 %copy-start.20 = (bf16[4,256,256]{2,1,0:T(8,128)(2,1)S(1)}, bf16[4,256,256]{2,1,0:T(8,128)(2,1)}, u32[]{:S(2)}) copy-start(bf16[4,256,256]{2,1,0:T(8,128)(2,1)} %slice.211) | copy-start | bytes 1572868
  168.0 57.0 %copy-start.21 = (f32[4,4,256]{2,1,0:T(4,128)S(1)}, f32[4,4,256]{2,1,0:T(4,128)}, u32[]{:S(2)}) copy-start(f32[4,4,256]{2,1,0:T(4,128)} %get-tuple-element.14.one_ref) | copy-start | bytes 49156
  170.7 54.3 %all-to-all-start.3 = ((bf16[4,256,256]{2,1,0:T(8,128)(2,1)}), bf16[4,256,256]{2,1,0:T(8,128)(2,1)S(1)}, u32[]{:S(2)}, u32[]{:S(2)}) async-start(bf16[4,256,256]{2,1,0:T(8,128)(2,1)} %bitcast.70), calls=%async_computation.3 | async-start | bytes 1048576 | tf_op jit(solution)/shard_map/all_to_all | solution.py:292
  (3 other events, 2.4 us)
Sparse Core Ops, SparseCore 0:
  18.8 67.7 all-gather.4

commit v2 on v1

--- a/solution.py
+++ b/solution.py
@@ -11,8 +11,8 @@
 NX, NZ, NY, NCORE = 4, 8, 4, 2
 ROWS = 256
 SLAB = 512
-QUARTER = 2048
-PACK = 80
+FIRST = (0, 0, 2, 3)
+VMEM_LIMIT = 58 * 1024 * 1024
 F32 = jnp.float32
 BF16 = jnp.bfloat16
 PRECISE = lax.Precision.HIGHEST
@@ -64,8 +64,9 @@
     final = responses[:, ::-1, :].transpose(0, 2, 1).astype(BF16)
     final = jnp.concatenate([final, jnp.zeros_like(final)], axis=1).reshape(classes * 8, CH)
     gains = gains.reshape(classes * 4, CH)
-    gains_hi = gains.astype(BF16)
-    gains_lo = (gains - gains_hi.astype(F32)).astype(BF16)
+    gains_hi = lax.reduce_precision(gains, 8, 7)
+    gains_lo = (gains - gains_hi).astype(BF16)
+    gains_hi = gains_hi.astype(BF16)
     gain_stack = jnp.concatenate([gains_hi, gains_lo, gains_hi], axis=0)
     power = powers[-1]
     power_two = jnp.einsum("kab,kbc->kac", power, power, precision=PRECISE)
@@ -83,23 +84,16 @@
     return out
 
 
-def factor_block(g_ref, s):
-    parts = [g_ref[s, :, 0:32, :]]
-    if s >= 1:
-        parts.append(g_ref[s, :, 32:64, :])
-    if s >= 2:
-        low = g_ref[1, :, 64:80, :] if s == 2 else g_ref[0, :, 32:48, :]
-        parts.append(jnp.concatenate([g_ref[s, :, 64:80, :], low], axis=1))
-    if s >= 3:
-        parts.append(g_ref[0, :, 48:80, :])
-    return jnp.concatenate([p.reshape(ROWS, CH) for p in parts], axis=1)
+def factor_block(g_refs, s):
+    parts = [g_refs[q][s - FIRST[q]].reshape(ROWS, CH) for q in range(s + 1)]
+    return jnp.concatenate(parts, axis=1) if s else parts[0]
 
 
 def product_kernel(blocks, has_acc, last, *refs):
     refs = list(refs)
     refs.pop(0)
     acc_ref = refs.pop(0) if has_acc else None
-    g_refs = [refs.pop(0) for _ in range(blocks)]
+    g_refs = [[refs.pop(0) for _ in range(NX)] for _ in range(blocks)]
     n_refs = [refs.pop(0) for _ in range(blocks)] if not last else [refs.pop(0), refs.pop(0)]
     if last:
         final_ref, onehot_ref, out_ref, end_ref = refs
@@ -137,8 +131,11 @@
     width = noise_blocks[0].shape[1]
     scalars = jnp.stack(where_z).astype(jnp.int32)
 
-    def g_spec(b):
-        return pl.BlockSpec((NX, 8, PACK, CH), lambda i, zs: (0, 0, 0, zs[b]))
+    def g_spec(b, q):
+        first, count = FIRST[q], NX - FIRST[q]
+        return pl.BlockSpec(
+            (count, 8, 32, CH), lambda i, zs: (first // count, 0, 0, q * NZ + zs[b])
+        )
 
     def whole(shape):
         return pl.BlockSpec(shape, lambda i, zs: (0,) * len(shape))
@@ -147,8 +144,8 @@
     if acc is not None:
         args.append(acc)
         specs.append(whole(acc.shape))
-    args += [gathered] * blocks
-    specs += [g_spec(b) for b in range(blocks)]
+    args += [gathered] * (blocks * NX)
+    specs += [g_spec(b, q) for b in range(blocks) for q in range(NX)]
     args += noise_blocks
     specs += [whole(n.shape) for n in noise_blocks]
     rows = NX * ROWS
@@ -169,7 +166,7 @@
             num_scalar_prefetch=1, grid=(1,), in_specs=specs, out_specs=out_specs
         ),
         out_shape=out_shape,
-        compiler_params=pltpu.CompilerParams(vmem_limit_bytes=40 * 1024 * 1024),
+        compiler_params=pltpu.CompilerParams(vmem_limit_bytes=VMEM_LIMIT),
         cost_estimate=pl.CostEstimate(
             flops=blocks * 2 * 10 * ROWS * CH * width,
             bytes_accessed=blocks * (1310720 + 524288) + 2097152,
@@ -234,7 +231,7 @@
             scratch_shapes=[pltpu.VMEM((4, ROWS), F32)],
         ),
         out_shape=jax.ShapeDtypeStruct((ROWS, NX * SLAB), F32),
-        compiler_params=pltpu.CompilerParams(vmem_limit_bytes=40 * 1024 * 1024),
+        compiler_params=pltpu.CompilerParams(vmem_limit_bytes=VMEM_LIMIT),
         cost_estimate=pl.CostEstimate(
             flops=8 * 2 * ROWS * CH * 1100, bytes_accessed=4 * 1024 * 1024, transcendentals=0
         ),
@@ -250,21 +247,21 @@
     z = lax.axis_index("z")
     tm = lax.axis_index("y") * NCORE + lax.axis_index("c")
 
-    mine = lax.dynamic_slice(factor, (tm * 32, 0), (32, factor.shape[1]))
-    quarter = [mine[:, q * QUARTER : (q + 1) * QUARTER] for q in range(4)]
-    surplus = jnp.concatenate([quarter[2][16:], quarter[3]], axis=0)
-    taken = lax.ppermute(surplus, "x", [(3, 0), (2, 1)])
-    share = jnp.concatenate(
-        [
-            quarter[0],
-            jnp.where(x == 0, taken[:32], quarter[1]),
-            jnp.where(x == 0, taken[32:48], jnp.where(x == 1, taken[:16], quarter[2][:16])),
-        ],
-        axis=0,
+    share = lax.dynamic_slice(factor, (tm * 32, 0), (32, factor.shape[1]))
+    gathered = lax.all_gather(share, ("x", "y", "c"))
+    gathered = gathered.reshape(NX, 8, 32, factor.shape[1])
+
+    own = []
+    for half in range(2):
+        first = half * CH
+        slabs = jnp.concatenate(
+            [white_noise[:, s * SLAB + first : s * SLAB + first + CH] for s in range(NX)], axis=0
+        )
+        own.append(lax.all_to_all(slabs, "x", 0, 0, tiled=True))
+
+    site_class, site_decay, site_angle, site_mix, own[1] = lax.optimization_barrier(
+        (site_class, site_decay, site_angle, site_mix, own[1])
     )
-    gathered = lax.all_gather(share, ("x", "y", "c"))
-    gathered = gathered.reshape(NX, 8, PACK, QUARTER)
-
     toeplitz, final, gain, power, power_two = tables(site_decay, site_angle, site_mix)
     by_block = site_class.reshape(NX, NZ, ROWS)
     ids = jnp.arange(4, dtype=jnp.int32)
@@ -274,16 +271,14 @@
     own_hot = (own_class == ids[:, None]).astype(F32)
     own_mask = (own_class.reshape(ROWS, 1) == ids[None, :]).astype(BF16)
 
-    cut = white_noise.reshape(ROWS, NX, 2, CH)
     excitation, ends = [], []
     for half in range(2):
-        slabs = cut[:, :, half, :].transpose(1, 0, 2).reshape(NX * ROWS, CH)
-        own = lax.all_to_all(slabs, "x", 0, 0, tiled=True)
-        up1, down1 = ring(own, 1), ring(own, -1)
+        up1, down1 = ring(own[half], 1), ring(own[half], -1)
         up2, down2 = ring(up1, 1), ring(down1, -1)
         up3, down3 = ring(up2, 1), ring(down2, -1)
+        total = product(None, gathered, [z, (z + 7) % 8, (z + 1) % 8], [own[half], up1, down1])
+        up3, down3, total = lax.optimization_barrier((up3, down3, total))
         up4, down4 = ring(up3[:512], 1), ring(down3[512:], -1)
-        total = product(None, gathered, [z, (z + 7) % 8, (z + 1) % 8], [own, up1, down1])
         total = product(total, gathered, [(z + 6) % 8, (z + 2) % 8], [up2, down2])
         total = product(total, gathered, [(z + 5) % 8, (z + 3) % 8], [up3, down3])
         local, end = product(total, gathered, [(z + 4) % 8], [up4, down4], (final, tile_hot))
@@ -292,8 +287,9 @@
             lax.all_to_all(local, "x", 0, 0, tiled=True).reshape(NX, ROWS, CH)
         )
     slab_end = apply_power(per_row(power, tile_hot), ends[0]) + ends[1]
-    all_ends = lax.all_gather(slab_end, ("y", "c", "x"))
-    own_ends = lax.dynamic_slice(all_ends, (0, 0, x * ROWS), (32, 4, ROWS))
+    to_send = slab_end.reshape(4, NX, ROWS).transpose(1, 0, 2)
+    to_send = jnp.tile(to_send, (NY * NCORE, 1, 1))
+    own_ends = lax.all_to_all(to_send, ("y", "c", "x"), 0, 0, tiled=True)
     return filtered(
         jnp.reshape(tm * NX, (1,)).astype(jnp.int32),
         excitation[0], excitation[1], own_ends, own_mask, own_hot,

time: 237 us -> 206 us (0.87)
  blocking collectives: 50 us -> 0 us
  local copies, waits for them, and re-layouts: 50.3 us -> 20.2 us
  waiting for transfers between devices: 37.8 us -> 59.9 us
  Pallas kernels: 24.1 us -> 42.7 us
  starting transfers between devices: 47.3 us -> 53.1 us
    all_gather x1 -> x0, blocking collectives: 50 us -> none  [body(): all_ends = lax.all_gather(slab_end, ('y', 'c', 'x'))]
    unnamed x63 -> x51, local copies, waits for them, and re-layouts: 27.7 us -> 1.89 us
    all_to_all x2 -> x3, waiting for transfers between devices: 0.01 us -> 19.7 us  [the longest x2 12.9 us: body(): own.append(lax.all_to_all(slabs, 'x', 0, 0, tiled=True))]
    pallas_call x8, Pallas kernels: 20.2 us -> 37.2 us  [product(): pl.pallas_call(functools.partial(product_kernel, blocks, acc is not None,...]
    all_to_all x2 -> x3, starting transfers between devices: 7.8 us -> 24.5 us  [the longest x1 16.2 us: body(): own_ends = lax.all_to_all(to_send, ('y', 'c', 'x'), 0, 0, tiled=True)]
    all_to_all x2, waiting for transfers between devices: 0.01 us -> 11.2 us  [body(): lax.all_to_all(local, 'x', 0, 0, tiled=True).reshape(NX, ROWS, CH)]
    ppermute x16, starting transfers between devices: 30 us -> 21.5 us  [ring(): return lax.ppermute(value, 'z', [(i, (i + by) % NZ) for i in range(NZ)])]
    ppermute x16, waiting for transfers between devices: 31.5 us -> 24.5 us  [ring(): return lax.ppermute(value, 'z', [(i, (i + by) % NZ) for i in range(NZ)])]
  transfers between devices with their start and end apart: 22 -> 22, of which waited for: 6 -> 10; matrix products, arithmetic and copies ran while one was open for 16% -> 15% of each run, Pallas kernels for 9% -> 17%
where the time goes in v2:
time: 206 us; the launch traced here: 205 us
  waiting for transfers between devices  59.9 us (29%)
  starting transfers between devices  53.1 us (26%)
  Pallas kernels  42.7 us (21%)
  local copies, waits for them, and re-layouts  20.2 us (10%)
  between operations  13.9 us (7%)
  other arithmetic  8.37 us (4%)
  matrix products  6.7 us (3%)
    pallas_call x8, Pallas kernels, product(): pl.pallas_call(functools.partial(product_kernel, blocks, acc is not None,...  37.2 us
    ppermute x16, waiting for transfers between devices, ring(): return lax.ppermute(value, 'z', [(i, (i + by) % NZ) for i in range(NZ)])  24.5 us
    ppermute x16, starting transfers between devices, ring(): return lax.ppermute(value, 'z', [(i, (i + by) % NZ) for i in range(NZ)])  21.5 us
    all_to_all x1, starting transfers between devices, body(): own_ends = lax.all_to_all(to_send, ('y', 'c', 'x'), 0, 0, tiled=True)  16.2 us
    all_to_all x2, waiting for transfers between devices, body(): own.append(lax.all_to_all(slabs, 'x', 0, 0, tiled=True))  12.9 us
    all_to_all x2, waiting for transfers between devices, body(): lax.all_to_all(local, 'x', 0, 0, tiled=True).reshape(NX, ROWS, CH)  11.2 us
    all_to_all x2, starting transfers between devices, body(): own.append(lax.all_to_all(slabs, 'x', 0, 0, tiled=True))  8.33 us
    all_to_all x2, starting transfers between devices, body(): lax.all_to_all(local, 'x', 0, 0, tiled=True).reshape(NX, ROWS, CH)  7.07 us
  transfers between devices with their start and end apart: 22, of which 10 were waited for; matrix products, arithmetic and copies ran while one was open for 15% of the time, Pallas kernels for 17%

profile of v2, /device:TPU:1, one launch (start us, length us, event | category | flops | bytes accessed | tf_op | source)
XLA Modules:
  0.0 204.9 jit_solution(14801862435060470442)
XLA Ops:
  6.5 1.9 constant_dynamic-slice_fusion.2
  8.5 1.4 fusion.44
  9.9 0.8 pad_maximum_fusion.1
  10.7 4.8 %all-to-all-start.1 = ((bf16[4,256,256]{2,1,0:T(8,128)(2,1)}), bf16[4,256,256]{2,1,0:T(8,128)(2,1)S(1)}, u32[]{:S(2)}, u32[]{:S(2)}) async-start(bf16[4,256,256]{2,1,0:T(8,128)(2,1)} %bitcast.13), calls=%async_computation.1 | async-start | bytes 1048576 | tf_op jit(solution)/shard_map/all_to_all | solution.py:260
  17.4 0.8 pad_maximum_fusion
  18.2 4.7 %all-to-all-done.1 = bf16[4,256,256]{2,1,0:T(8,128)(2,1)S(1)} async-done(((bf16[4,256,256]{2,1,0:T(8,128)(2,1)}), bf16[4,256,256]{2,1,0:T(8,128)(2,1)S(1)}, u32[]{:S(2)}, u32[]{:S(2)}) %all-to-all-start.1) | async-done | bytes 524320 | tf_op jit(solution)/shard_map/all_to_all | solution.py:260
  22.9 3.5 %all-to-all-start = ((bf16[4,256,256]{2,1,0:T(8,128)(2,1)}), bf16[4,256,256]{2,1,0:T(8,128)(2,1)S(1)}, u32[]{:S(2)}, u32[]{:S(2)}) async-start(bf16[4,256,256]{2,1,0:T(8,128)(2,1)} %bitcast.7), calls=%async_computation | async-start | bytes 1048576 | tf_op jit(solution)/shard_map/all_to_all | solution.py:260
  29.0 1.0 convolution_bitcast_fusion.4
  32.4 8.2 %all-to-all-done = bf16[4,256,256]{2,1,0:T(8,128)(2,1)S(1)} async-done(((bf16[4,256,256]{2,1,0:T(8,128)(2,1)}), bf16[4,256,256]{2,1,0:T(8,128)(2,1)S(1)}, u32[]{:S(2)}, u32[]{:S(2)}) %all-to-all-start) | async-done | bytes 524320 | tf_op jit(solution)/shard_map/all_to_all | solution.py:260
  40.6 3.7 %collective-permute-start.3 = (bf16[1024,256]{1,0:T(8,128)(2,1)S(1)}, bf16[1024,256]{1,0:T(8,128)(2,1)}, u32[]{:S(2)}, u32[]{:S(2)}) collective-permute-start(bf16[1024,256]{1,0:T(8,128)(2,1)S(1)} %bitcast.285), channel_id=1, source_target_pairs={{0,56},{8,0},{16,8},{24,16},{32,24},{40,32},{48,40},{56,48},{1,57}... | collective-permute-start | bytes 1572872 | tf_op jit(solution)/shard_map/ppermute | solution.py:242
  44.3 2.7 %collective-permute-start.11 = (bf16[1024,256]{1,0:T(8,128)(2,1)S(1)}, bf16[1024,256]{1,0:T(8,128)(2,1)}, u32[]{:S(2)}, u32[]{:S(2)}) collective-permute-start(bf16[1024,256]{1,0:T(8,128)(2,1)S(1)} %bitcast.282), channel_id=1, source_target_pairs={{0,56},{8,0},{16,8},{24,16},{32,24},{40,32},{48,40},{56,48},{1,57}... | collective-permute-start | bytes 1572872 | tf_op jit(solution)/shard_map/ppermute | solution.py:242
  48.2 0.8 copy.159
  49.4 3.4 %fusion.47 = f32[4,1,256,4]{1,2,3,0:T(8,128)S(1)} fusion(f32[256,4,4,4]{0,2,3,1:T(4,128)S(1)} %concatenate.58, f32[4,4,1,1]{1,2,3,0:T(1,128)S(1)} %bitcast.306), kind=kOutput, calls=%fused_computation.106 | convolution fusion | flops 196608 | bytes 81984 | tf_op jit(solution)/shard_map/ka,jkab->kbj/dot_general | solution.py:55
  53.5 2.8 %collective-permute-start.4 = (bf16[1024,256]{1,0:T(8,128)(2,1)}, bf16[1024,256]{1,0:T(8,128)(2,1)}, u32[]{:S(2)}, u32[]{:S(2)}) collective-permute-start(bf16[1024,256]{1,0:T(8,128)(2,1)} %collective-permute-done.3.refs_15_), channel_id=1, source_target_pairs={{0,56},{8,0},{16,8},{24,16},{32,24},{40,32},{48,40},{56,48},{1,57}... | collective-permute-start | bytes 1572872 | tf_op jit(solution)/shard_map/ppermute | solution.py:242
  56.3 7.6 %collective-permute-done.11.refs_15_ = bf16[1024,256]{1,0:T(8,128)(2,1)} collective-permute-done((bf16[1024,256]{1,0:T(8,128)(2,1)S(1)}, bf16[1024,256]{1,0:T(8,128)(2,1)}, u32[]{:S(2)}, u32[]{:S(2)}) %collective-permute-start.11) | collective-permute-done | bytes 524320 | tf_op jit(solution)/shard_map/ppermute | solution.py:242
  63.9 2.2 %collective-permute-start.12 = (bf16[1024,256]{1,0:T(8,128)(2,1)}, bf16[1024,256]{1,0:T(8,128)(2,1)}, u32[]{:S(2)}, u32[]{:S(2)}) collective-permute-start(bf16[1024,256]{1,0:T(8,128)(2,1)} %collective-permute-done.11.refs_15_), channel_id=1, source_target_pairs={{0,56},{8,0},{16,8},{24,16},{32,24},{40,32},{48,40},{56,48},{1,57}... | collective-permute-start | bytes 1572872 | tf_op jit(solution)/shard_map/ppermute | solution.py:242
  66.9 8.2 %collective-permute-done.4.refs_11_ = bf16[1024,256]{1,0:T(8,128)(2,1)} collective-permute-done((bf16[1024,256]{1,0:T(8,128)(2,1)}, bf16[1024,256]{1,0:T(8,128)(2,1)}, u32[]{:S(2)}, u32[]{:S(2)}) %collective-permute-start.4) | collective-permute-done | bytes 524320 | tf_op jit(solution)/shard_map/ppermute | solution.py:242
  75.1 2.2 %collective-permute-start.5 = (bf16[1024,256]{1,0:T(8,128)(2,1)}, bf16[1024,256]{1,0:T(8,128)(2,1)S(1)}, u32[]{:S(2)}, u32[]{:S(2)}) collective-permute-start(bf16[1024,256]{1,0:T(8,128)(2,1)} %collective-permute-done.4.refs_11_), channel_id=1, source_target_pairs={{0,56},{8,0},{16,8},{24,16},{32,24},{40,32},{48,40},{56,48},{1,57}... | collective-permute-start | bytes 1572872 | tf_op jit(solution)/shard_map/ppermute | solution.py:242
  77.3 0.9 multiply_reduce_fusion
  78.2 8.1 %collective-permute-done.12.refs_11_ = bf16[1024,256]{1,0:T(8,128)(2,1)} collective-permute-done((bf16[1024,256]{1,0:T(8,128)(2,1)}, bf16[1024,256]{1,0:T(8,128)(2,1)}, u32[]{:S(2)}, u32[]{:S(2)}) %collective-permute-start.12) | collective-permute-done | bytes 524320 | tf_op jit(solution)/shard_map/ppermute | solution.py:242
  86.4 2.2 %collective-permute-start.13 = (bf16[1024,256]{1,0:T(8,128)(2,1)}, bf16[1024,256]{1,0:T(8,128)(2,1)S(1)}, u32[]{:S(2)}, u32[]{:S(2)}) collective-permute-start(bf16[1024,256]{1,0:T(8,128)(2,1)} %collective-permute-done.12.refs_11_), channel_id=1, source_target_pairs={{0,56},{8,0},{16,8},{24,16},{32,24},{40,32},{48,40},{56,48},{1,57}... | collective-permute-start | bytes 1572872 | tf_op jit(solution)/shard_map/ppermute | solution.py:242
  89.8 4.6 %all-gather.3.cloned.1.call-done = bf16[1024,8192]{1,0:T(8,128)(2,1)} async-done(((bf16[32,8192]{1,0:T(8,128)(2,1)}), bf16[1024,8192]{1,0:T(8,128)(2,1)}) %all-gather.3.cloned.1.call-update) | async-done | bytes 16777232 | tf_op jit(solution)/shard_map/all_gather | solution.py:251
  94.4 5.5 %shard_map.64.refs_1_ = f32[1024,256]{1,0:T(8,128)} custom-call(s32[3]{0:T(128)} %pad_add_fusion.2.refs_0_, bf16[4,8,32,8192]{3,2,1,0:T(8,128)(2,1)} %bitcast.228, bf16[4,8,32,8192]{3,2,1,0:T(8,128)(2,1)} %bitcast.218, bf16[4,8,32,8192]{3,2,1,0:T(8,128)(2,1)} %bitcast.219, bf16[4,8,32,8192]{3,2,1,0:T(8,128)(2,1)} %bitcast.220, ...), custom_call_target="tpu_custom_call" | custom-call | flops 1006632960 | bytes 7602176 | tf_op jit(solution)/shard_map/pallas_call | solution.py:163
  100.0 0.8 slice.142
  101.5 1.3 collective-permute-start.6
  102.8 1.8 collective-permute-start.7
  104.5 5.6 %shard_map.68.refs_1_ = f32[1024,256]{1,0:T(8,128)} custom-call(s32[3]{0:T(128)} %pad_add_fusion.2.refs_0_, bf16[4,8,32,8192]{3,2,1,0:T(8,128)(2,1)} %bitcast.229, bf16[4,8,32,8192]{3,2,1,0:T(8,128)(2,1)} %bitcast.230, bf16[4,8,32,8192]{3,2,1,0:T(8,128)(2,1)} %bitcast.231, bf16[4,8,32,8192]{3,2,1,0:T(8,128)(2,1)} %bitcast.232, ...), custom_call_target="tpu_custom_call" | custom-call | flops 1006632960 | bytes 7602176 | tf_op jit(solution)/shard_map/pallas_call | solution.py:163
  110.7 0.8 slice.162
  112.2 2.7 %collective-permute-start.15 = (bf16[512,256]{1,0:T(8,128)(2,1)}, bf16[512,256]{1,0:T(8,128)(2,1)}, u32[]{:S(2)}, u32[]{:S(2)}) collective-permute-start(bf16[512,256]{1,0:T(8,128)(2,1)} %slice.162), channel_id=1, source_target_pairs={{0,56},{8,0},{16,8},{24,16},{32,24},{40,32},{48,40},{56,48},{1,57}... | collective-permute-start | bytes 786440 | tf_op jit(solution)/shard_map/ppermute | solution.py:242
  114.9 4.9 %shard_map.65.refs_1_ = f32[1024,256]{1,0:T(8,128)} custom-call(s32[2]{0:T(128)} %pad_add_fusion.1.refs_0_, f32[1024,256]{1,0:T(8,128)} %shard_map.64.refs_1_, bf16[4,8,32,8192]{3,2,1,0:T(8,128)(2,1)} %bitcast.248, bf16[4,8,32,8192]{3,2,1,0:T(8,128)(2,1)} %bitcast.242, bf16[4,8,32,8192]{3,2,1,0:T(8,128)(2,1)} %bitcast.243, ...), custom_call_target="tpu_custom_call" | custom-call | flops 671088640 | bytes 5767168 | tf_op jit(solution)/shard_map/pallas_call | solution.py:163
  119.8 4.9 %shard_map.66.refs_1_ = f32[1024,256]{1,0:T(8,128)} custom-call(s32[2]{0:T(128)} %pad_add_fusion.refs_0_, f32[1024,256]{1,0:T(8,128)} %shard_map.65.refs_1_, bf16[4,8,32,8192]{3,2,1,0:T(8,128)(2,1)} %bitcast.249, bf16[4,8,32,8192]{3,2,1,0:T(8,128)(2,1)} %bitcast.250, bf16[4,8,32,8192]{3,2,1,0:T(8,128)(2,1)} %bitcast.251, bf16[4,8,32,8192]{3,2,1,0:T(8,128)(2,1)} %bitcast.252, ...), custom_call_target="tpu_custom_call" | custom-call | flops 671088640 | bytes 5767168 | tf_op jit(solution)/shard_map/pallas_call | solution.py:163
  124.7 4.9 %shard_map.69.refs_1_ = f32[1024,256]{1,0:T(8,128)} custom-call(s32[2]{0:T(128)} %pad_add_fusion.1.refs_0_, f32[1024,256]{1,0:T(8,128)} %shard_map.68.refs_1_, bf16[4,8,32,8192]{3,2,1,0:T(8,128)(2,1)} %bitcast.261, bf16[4,8,32,8192]{3,2,1,0:T(8,128)(2,1)} %bitcast.258, bf16[4,8,32,8192]{3,2,1,0:T(8,128)(2,1)} %bitcast.259, ...), custom_call_target="tpu_custom_call" | custom-call | flops 671088640 | bytes 5767168 | tf_op jit(solution)/shard_map/pallas_call | solution.py:163
  129.6 4.9 %shard_map.70.refs_1_ = f32[1024,256]{1,0:T(8,128)} custom-call(s32[2]{0:T(128)} %pad_add_fusion.refs_0_, f32[1024,256]{1,0:T(8,128)} %shard_map.69.refs_1_, bf16[4,8,32,8192]{3,2,1,0:T(8,128)(2,1)} %bitcast.265, bf16[4,8,32,8192]{3,2,1,0:T(8,128)(2,1)} %bitcast.266, bf16[4,8,32,8192]{3,2,1,0:T(8,128)(2,1)} %bitcast.267, bf16[4,8,32,8192]{3,2,1,0:T(8,128)(2,1)} %bitcast.268, ...), custom_call_target="tpu_custom_call" | custom-call | flops 671088640 | bytes 5767168 | tf_op jit(solution)/shard_map/pallas_call | solution.py:163
  134.6 3.2 %shard_map.67 = (bf16[1024,256]{1,0:T(8,128)(2,1)}, f32[8,1024]{1,0:T(8,128)}) custom-call(s32[1]{0:T(128)} %bitcast.2.refs_0_, f32[1024,256]{1,0:T(8,128)} %shard_map.66.refs_1_, bf16[4,8,32,8192]{3,2,1,0:T(8,128)(2,1)} %bitcast.273, bf16[4,8,32,8192]{3,2,1,0:T(8,128)(2,1)} %bitcast.274, bf16[4,8,32,8192]{3,2,1,0:T(8,128)(2,1)} %bitcast.275, ...), custom_call_target="tpu_custom_call" | custom-call | flops 335544320 | bytes 3932160 | tf_op jit(solution)/shard_map/pallas_call | solution.py:163
  137.8 0.9 fusion.45
  138.8 3.2 %shard_map.71 = (bf16[1024,256]{1,0:T(8,128)(2,1)}, f32[8,1024]{1,0:T(8,128)}) custom-call(s32[1]{0:T(128)} %bitcast.2.refs_0_, f32[1024,256]{1,0:T(8,128)} %shard_map.70.refs_1_, bf16[4,8,32,8192]{3,2,1,0:T(8,128)(2,1)} %bitcast.277, bf16[4,8,32,8192]{3,2,1,0:T(8,128)(2,1)} %bitcast.278, bf16[4,8,32,8192]{3,2,1,0:T(8,128)(2,1)} %bitcast.279, ...), custom_call_target="tpu_custom_call" | custom-call | flops 335544320 | bytes 3932160 | tf_op jit(solution)/shard_map/pallas_call | solution.py:163
  142.0 0.8 fusion.12
  143.5 16.2 %all-to-all-start.4 = ((f32[32,4,256]{2,1,0:T(4,128)}), f32[32,4,256]{2,1,0:T(4,128)S(1)}, u32[]{:S(2)}, u32[]{:S(2)}) async-start(f32[32,4,256]{2,1,0:T(4,128)} %bitcast.81), calls=%async_computation.4 | async-start | bytes 262144 | tf_op jit(solution)/shard_map/all_to_all | solution.py:292
  160.6 6.7 %all-to-all-done.4.slabs_ref = f32[32,4,256]{2,1,0:T(4,128)S(1)} async-done(((f32[32,4,256]{2,1,0:T(4,128)}), f32[32,4,256]{2,1,0:T(4,128)S(1)}, u32[]{:S(2)}, u32[]{:S(2)}) %all-to-all-start.4) | async-done | bytes 131104 | tf_op jit(solution)/shard_map/all_to_all | solution.py:292
  167.3 3.5 %all-to-all-start.2 = ((bf16[4,256,256]{2,1,0:T(8,128)(2,1)}), bf16[4,256,256]{2,1,0:T(8,128)(2,1)S(1)}, u32[]{:S(2)}, u32[]{:S(2)}) async-start(bf16[4,256,256]{2,1,0:T(8,128)(2,1)} %bitcast.67), calls=%async_computation.2 | async-start | bytes 1048576 | tf_op jit(solution)/shard_map/all_to_all | solution.py:287
  170.9 9.1 %all-to-all-done.2.first_ref = bf16[4,256,256]{2,1,0:T(8,128)(2,1)S(1)} async-done(((bf16[4,256,256]{2,1,0:T(8,128)(2,1)}), bf16[4,256,256]{2,1,0:T(8,128)(2,1)S(1)}, u32[]{:S(2)}, u32[]{:S(2)}) %all-to-all-start.2) | async-done | bytes 524320 | tf_op jit(solution)/shard_map/all_to_all | solution.py:287
  180.1 3.6 %all-to-all-start.3 = ((bf16[4,256,256]{2,1,0:T(8,128)(2,1)}), bf16[4,256,256]{2,1,0:T(8,128)(2,1)S(1)}, u32[]{:S(2)}, u32[]{:S(2)}) async-start(bf16[4,256,256]{2,1,0:T(8,128)(2,1)} %bitcast.288), calls=%async_computation.3 | async-start | bytes 1048576 | tf_op jit(solution)/shard_map/all_to_all | solution.py:287
  184.4 0.8 copy.191
  185.6 1.8 reshape.364
  187.4 0.8 slice.191
  189.7 2.1 %all-to-all-done.3.second_ref = bf16[4,256,256]{2,1,0:T(8,128)(2,1)S(1)} async-done(((bf16[4,256,256]{2,1,0:T(8,128)(2,1)}), bf16[4,256,256]{2,1,0:T(8,128)(2,1)S(1)}, u32[]{:S(2)}, u32[]{:S(2)}) %all-to-all-start.3) | async-done | bytes 524320 | tf_op jit(solution)/shard_map/all_to_all | solution.py:287
  191.8 0.8 copy-done.8
  192.6 5.5 %shard_map.72 = f32[256,2048]{1,0:T(8,128)} custom-call(s32[1]{0:T(128)} %bitcast.1.place, bf16[4,256,256]{2,1,0:T(8,128)(2,1)} %copy-done.7, bf16[4,256,256]{2,1,0:T(8,128)(2,1)} %copy-done.8, f32[32,4,256]{2,1,0:T(4,128)} %copy-done.11, bf16[256,4]{1,0:T(8,128)(2,1)} %fusion.mask_ref, f32[4,256]{1,0:T(4,128)} %copy-done.19, ...), custom_call_target="tpu_custom_call" | custom-call | flops 1153433600 | bytes 4194304 | tf_op jit(solution)/shard_map/pallas_call | solution.py:224
  (149 shorter events, 17.3 us)
Async XLA Ops:
  6.5 20.0 %copy-start.20 = (f32[4,4]{1,0:T(4,128)S(1)}, f32[4,4]{1,0:T(4,128)}, u32[]{:S(2)}) copy-start(f32[4,4]{1,0:T(4,128)} %param.11) | copy-start | bytes 196
  6.5 19.9 %copy-start.22 = (f32[2,4]{1,0:T(2,128)S(1)}, f32[2,4]{1,0:T(2,128)}, u32[]{:S(2)}) copy-start(f32[2,4]{1,0:T(2,128)} %param.10) | copy-start | bytes 100
  6.5 19.9 %copy-start.23 = (f32[2,4]{1,0:T(2,128)S(1)}, f32[2,4]{1,0:T(2,128)}, u32[]{:S(2)}) copy-start(f32[2,4]{1,0:T(2,128)} %param.9) | copy-start | bytes 100
  6.5 87.9 %all-gather.3.cloned.1.call-start = ((), (), s32[]{:S(2)}) async-start(), calls=%async_computation.5 | async-start | bytes 17301504 | tf_op jit(solution)/shard_map/all_gather | solution.py:251
  9.8 39.3 %copy-start.16 = (s32[8192]{0:T(1024)S(1)}, s32[8192]{0:T(1024)}, u32[]{:S(2)}) copy-start(s32[8192]{0:T(1024)} %param.8) | copy-start | bytes 98308
  10.7 12.2 %all-to-all-start.1 = ((bf16[4,256,256]{2,1,0:T(8,128)(2,1)}), bf16[4,256,256]{2,1,0:T(8,128)(2,1)S(1)}, u32[]{:S(2)}, u32[]{:S(2)}) async-start(bf16[4,256,256]{2,1,0:T(8,128)(2,1)} %bitcast.13), calls=%async_computation.1 | async-start | bytes 1048576 | tf_op jit(solution)/shard_map/all_to_all | solution.py:260
  22.9 30.6 %copy-start = (bf16[4,256,256]{2,1,0:T(8,128)(2,1)}, bf16[4,256,256]{2,1,0:T(8,128)(2,1)S(1)}, u32[]{:S(2)}) copy-start(bf16[4,256,256]{2,1,0:T(8,128)(2,1)S(1)} %all-to-all-done.1) | copy-start | bytes 1572868
  22.9 17.7 %all-to-all-start = ((bf16[4,256,256]{2,1,0:T(8,128)(2,1)}), bf16[4,256,256]{2,1,0:T(8,128)(2,1)S(1)}, u32[]{:S(2)}, u32[]{:S(2)}) async-start(bf16[4,256,256]{2,1,0:T(8,128)(2,1)} %bitcast.7), calls=%async_computation | async-start | bytes 1048576 | tf_op jit(solution)/shard_map/all_to_all | solution.py:260
  40.6 53.8 %copy-start.1 = (bf16[4,256,256]{2,1,0:T(8,128)(2,1)}, bf16[4,256,256]{2,1,0:T(8,128)(2,1)S(1)}, u32[]{:S(2)}) copy-start(bf16[4,256,256]{2,1,0:T(8,128)(2,1)S(1)} %all-to-all-done) | copy-start | bytes 1572868
  40.6 12.9 %collective-permute-start.3 = (bf16[1024,256]{1,0:T(8,128)(2,1)S(1)}, bf16[1024,256]{1,0:T(8,128)(2,1)}, u32[]{:S(2)}, u32[]{:S(2)}) collective-permute-start(bf16[1024,256]{1,0:T(8,128)(2,1)S(1)} %bitcast.285), channel_id=1, source_target_pairs={{0,56},{8,0},{16,8},{24,16},{32,24},{40,32},{48,40},{56,48},{1,57}... | collective-permute-start | bytes 1572872 | tf_op jit(solution)/shard_map/ppermute | solution.py:242
  44.3 11.9 %collective-permute-start = (bf16[1024,256]{1,0:T(8,128)(2,1)S(1)}, bf16[1024,256]{1,0:T(8,128)(2,1)}, u32[]{:S(2)}, u32[]{:S(2)}) collective-permute-start(bf16[1024,256]{1,0:T(8,128)(2,1)S(1)} %bitcast.286), channel_id=1, source_target_pairs={{0,8},{8,16},{16,24},{24,32},{32,40},{40,48},{48,56},{56,0},{1,9},... | collective-permute-start | bytes 1572872 | tf_op jit(solution)/shard_map/ppermute | solution.py:242
  44.3 19.5 %collective-permute-start.11 = (bf16[1024,256]{1,0:T(8,128)(2,1)S(1)}, bf16[1024,256]{1,0:T(8,128)(2,1)}, u32[]{:S(2)}, u32[]{:S(2)}) collective-permute-start(bf16[1024,256]{1,0:T(8,128)(2,1)S(1)} %bitcast.282), channel_id=1, source_target_pairs={{0,56},{8,0},{16,8},{24,16},{32,24},{40,32},{48,40},{56,48},{1,57}... | collective-permute-start | bytes 1572872 | tf_op jit(solution)/shard_map/ppermute | solution.py:242
  47.0 19.1 %collective-permute-start.8 = (bf16[1024,256]{1,0:T(8,128)(2,1)S(1)}, bf16[1024,256]{1,0:T(8,128)(2,1)}, u32[]{:S(2)}, u32[]{:S(2)}) collective-permute-start(bf16[1024,256]{1,0:T(8,128)(2,1)S(1)} %bitcast.283), channel_id=1, source_target_pairs={{0,8},{8,16},{16,24},{24,32},{32,40},{40,48},{48,56},{56,0},{1,9},... | collective-permute-start | bytes 1572872 | tf_op jit(solution)/shard_map/ppermute | solution.py:242
  48.2 30.0 %copy-start.12 = (f32[1,4,4,4]{1,2,3,0:T(4,128)}, f32[1,4,4,4]{1,2,3,0:T(4,128)S(1)}, u32[]{:S(2)}) copy-start(f32[1,4,4,4]{1,2,3,0:T(4,128)S(1)} %copy.187) | copy-start | bytes 772
  49.1 29.1 %copy-start.14 = (s32[4,8,256]{2,1,0:T(8,128)}, s32[4,8,256]{2,1,0:T(8,128)S(1)}, u32[]{:S(2)}) copy-start(s32[4,8,256]{2,1,0:T(8,128)S(1)} %reshape.362) | copy-start | bytes 98308
  53.5 21.6 %collective-permute-start.4 = (bf16[1024,256]{1,0:T(8,128)(2,1)}, bf16[1024,256]{1,0:T(8,128)(2,1)}, u32[]{:S(2)}, u32[]{:S(2)}) collective-permute-start(bf16[1024,256]{1,0:T(8,128)(2,1)} %collective-permute-done.3.refs_15_), channel_id=1, source_target_pairs={{0,56},{8,0},{16,8},{24,16},{32,24},{40,32},{48,40},{56,48},{1,57}... | collective-permute-start | bytes 1572872 | tf_op jit(solution)/shard_map/ppermute | solution.py:242
  56.3 21.1 %collective-permute-start.1 = (bf16[1024,256]{1,0:T(8,128)(2,1)}, bf16[1024,256]{1,0:T(8,128)(2,1)}, u32[]{:S(2)}, u32[]{:S(2)}) collective-permute-start(bf16[1024,256]{1,0:T(8,128)(2,1)} %collective-permute-done.refs_14_), channel_id=1, source_target_pairs={{0,8},{8,16},{16,24},{24,32},{32,40},{40,48},{48,56},{56,0},{1,9},... | collective-permute-start | bytes 1572872 | tf_op jit(solution)/shard_map/ppermute | solution.py:242
  63.9 22.5 %collective-permute-start.12 = (bf16[1024,256]{1,0:T(8,128)(2,1)}, bf16[1024,256]{1,0:T(8,128)(2,1)}, u32[]{:S(2)}, u32[]{:S(2)}) collective-permute-start(bf16[1024,256]{1,0:T(8,128)(2,1)} %collective-permute-done.11.refs_15_), channel_id=1, source_target_pairs={{0,56},{8,0},{16,8},{24,16},{32,24},{40,32},{48,40},{56,48},{1,57}... | collective-permute-start | bytes 1572872 | tf_op jit(solution)/shard_map/ppermute | solution.py:242
  66.1 22.5 %collective-permute-start.9 = (bf16[1024,256]{1,0:T(8,128)(2,1)}, bf16[1024,256]{1,0:T(8,128)(2,1)S(1)}, u32[]{:S(2)}, u32[]{:S(2)}) collective-permute-start(bf16[1024,256]{1,0:T(8,128)(2,1)} %collective-permute-done.8.refs_14_), channel_id=1, source_target_pairs={{0,8},{8,16},{16,24},{24,32},{32,40},{40,48},{48,56},{56,0},{1,9},... | collective-permute-start | bytes 1572872 | tf_op jit(solution)/shard_map/ppermute | solution.py:242
  66.1 12.1 %copy-start.9 = (f32[4,1024]{1,0:T(4,128)}, f32[4,1024]{1,0:T(4,128)S(1)}, u32[]{:S(2)}) copy-start(f32[4,1024]{1,0:T(4,128)S(1)} %fusion.21.refs_9_) | copy-start | bytes 49156
  75.1 24.8 %collective-permute-start.5 = (bf16[1024,256]{1,0:T(8,128)(2,1)}, bf16[1024,256]{1,0:T(8,128)(2,1)S(1)}, u32[]{:S(2)}, u32[]{:S(2)}) collective-permute-start(bf16[1024,256]{1,0:T(8,128)(2,1)} %collective-permute-done.4.refs_11_), channel_id=1, source_target_pairs={{0,56},{8,0},{16,8},{24,16},{32,24},{40,32},{48,40},{56,48},{1,57}... | collective-permute-start | bytes 1572872 | tf_op jit(solution)/shard_map/ppermute | solution.py:242
  77.3 22.6 %collective-permute-start.2 = (bf16[1024,256]{1,0:T(8,128)(2,1)}, bf16[1024,256]{1,0:T(8,128)(2,1)S(1)}, u32[]{:S(2)}, u32[]{:S(2)}) collective-permute-start(bf16[1024,256]{1,0:T(8,128)(2,1)} %collective-permute-done.1.refs_10_), channel_id=1, source_target_pairs={{0,8},{8,16},{16,24},{24,32},{32,40},{40,48},{48,56},{56,0},{1,9},... | collective-permute-start | bytes 1572872 | tf_op jit(solution)/shard_map/ppermute | solution.py:242
  86.4 23.8 %collective-permute-start.13 = (bf16[1024,256]{1,0:T(8,128)(2,1)}, bf16[1024,256]{1,0:T(8,128)(2,1)S(1)}, u32[]{:S(2)}, u32[]{:S(2)}) collective-permute-start(bf16[1024,256]{1,0:T(8,128)(2,1)} %collective-permute-done.12.refs_11_), channel_id=1, source_target_pairs={{0,56},{8,0},{16,8},{24,16},{32,24},{40,32},{48,40},{56,48},{1,57}... | collective-permute-start | bytes 1572872 | tf_op jit(solution)/shard_map/ppermute | solution.py:242
  88.6 11.4 %copy-start.6 = (bf16[1024,256]{1,0:T(8,128)(2,1)}, bf16[1024,256]{1,0:T(8,128)(2,1)S(1)}, u32[]{:S(2)}) copy-start(bf16[1024,256]{1,0:T(8,128)(2,1)S(1)} %collective-permute-done.9.refs_10_) | copy-start | bytes 1572868
  88.6 22.1 %collective-permute-start.10 = (bf16[1024,256]{1,0:T(8,128)(2,1)S(1)}, bf16[1024,256]{1,0:T(8,128)(2,1)S(1)}, u32[]{:S(2)}, u32[]{:S(2)}) collective-permute-start(bf16[1024,256]{1,0:T(8,128)(2,1)S(1)} %collective-permute-done.9.refs_10_), channel_id=1, source_target_pairs={{0,8},{8,16},{16,24},{24,32},{32,40},{40,48},{48,56},{56,0},{1,9},... | collective-permute-start | bytes 1572872 | tf_op jit(solution)/shard_map/ppermute | solution.py:242
  100.0 10.2 %copy-start.2 = (bf16[1024,256]{1,0:T(8,128)(2,1)}, bf16[1024,256]{1,0:T(8,128)(2,1)S(1)}, u32[]{:S(2)}) copy-start(bf16[1024,256]{1,0:T(8,128)(2,1)S(1)} %collective-permute-done.5.refs_11_) | copy-start | bytes 1572868
  100.0 10.1 %copy-start.4 = (bf16[1024,256]{1,0:T(8,128)(2,1)}, bf16[1024,256]{1,0:T(8,128)(2,1)S(1)}, u32[]{:S(2)}) copy-start(bf16[1024,256]{1,0:T(8,128)(2,1)S(1)} %collective-permute-done.2.refs_10_) | copy-start | bytes 1572868
  101.5 33.1 %collective-permute-start.6 = (bf16[512,256]{1,0:T(8,128)(2,1)}, bf16[512,256]{1,0:T(8,128)(2,1)}, u32[]{:S(2)}, u32[]{:S(2)}) collective-permute-start(bf16[512,256]{1,0:T(8,128)(2,1)} %slice.141), channel_id=1, source_target_pairs={{0,8},{8,16},{16,24},{24,32},{32,40},{40,48},{48,56},{56,0},{1,9},... | collective-permute-start | bytes 786440 | tf_op jit(solution)/shard_map/ppermute | solution.py:242
  102.8 31.8 %collective-permute-start.7 = (bf16[512,256]{1,0:T(8,128)(2,1)}, bf16[512,256]{1,0:T(8,128)(2,1)}, u32[]{:S(2)}, u32[]{:S(2)}) collective-permute-start(bf16[512,256]{1,0:T(8,128)(2,1)} %slice.142), channel_id=1, source_target_pairs={{0,56},{8,0},{16,8},{24,16},{32,24},{40,32},{48,40},{56,48},{1,57}... | collective-permute-start | bytes 786440 | tf_op jit(solution)/shard_map/ppermute | solution.py:242
  110.1 9.7 %copy-start.3 = (bf16[1024,256]{1,0:T(8,128)(2,1)}, bf16[1024,256]{1,0:T(8,128)(2,1)S(1)}, u32[]{:S(2)}) copy-start(bf16[1024,256]{1,0:T(8,128)(2,1)S(1)} %collective-permute-done.13.refs_11_) | copy-start | bytes 1572868
  110.7 9.1 %copy-start.5 = (bf16[1024,256]{1,0:T(8,128)(2,1)}, bf16[1024,256]{1,0:T(8,128)(2,1)S(1)}, u32[]{:S(2)}) copy-start(bf16[1024,256]{1,0:T(8,128)(2,1)S(1)} %collective-permute-done.10.refs_10_) | copy-start | bytes 1572868
  112.2 26.6 %collective-permute-start.14 = (bf16[512,256]{1,0:T(8,128)(2,1)}, bf16[512,256]{1,0:T(8,128)(2,1)}, u32[]{:S(2)}, u32[]{:S(2)}) collective-permute-start(bf16[512,256]{1,0:T(8,128)(2,1)} %slice.161), channel_id=1, source_target_pairs={{0,8},{8,16},{16,24},{24,32},{32,40},{40,48},{48,56},{56,0},{1,9},... | collective-permute-start | bytes 786440 | tf_op jit(solution)/shard_map/ppermute | solution.py:242
  112.2 26.6 %collective-permute-start.15 = (bf16[512,256]{1,0:T(8,128)(2,1)}, bf16[512,256]{1,0:T(8,128)(2,1)}, u32[]{:S(2)}, u32[]{:S(2)}) collective-permute-start(bf16[512,256]{1,0:T(8,128)(2,1)} %slice.162), channel_id=1, source_target_pairs={{0,56},{8,0},{16,8},{24,16},{32,24},{40,32},{48,40},{56,48},{1,57}... | collective-permute-start | bytes 786440 | tf_op jit(solution)/shard_map/ppermute | solution.py:242
  138.7 3.3 %copy-start.10 = (f32[4,4,1024]{2,1,0:T(4,128)S(1)}, f32[4,4,1024]{2,1,0:T(4,128)}, u32[]{:S(2)}) copy-start(f32[4,4,1024]{2,1,0:T(4,128)} %multiply_reduce_fusion) | copy-start | bytes 196612
  138.7 21.0 %copy-start.15 = (f32[1,4,4,4]{3,2,1,0:T(4,128)S(1)}, f32[1,4,4,4]{3,2,1,0:T(4,128)}, u32[]{:S(2)}) copy-start(f32[1,4,4,4]{3,2,1,0:T(4,128)} %copy.159) | copy-start | bytes 772
  138.8 32.1 %copy-start.21 = (bf16[4,1,256]{2,1,0:T(2,128)(2,1)S(1)}, bf16[4,1,256]{2,1,0:T(2,128)(2,1)}, u32[]{:S(2)}) copy-start(bf16[4,1,256]{2,1,0:T(2,128)(2,1)} %fusion.46) | copy-start | bytes 6148
  138.8 44.9 %copy-start.17 = (bf16[16,256]{1,0:T(8,128)(2,1)S(1)}, bf16[16,256]{1,0:T(8,128)(2,1)}, u32[]{:S(2)}) copy-start(bf16[16,256]{1,0:T(8,128)(2,1)} %get-tuple-element.55) | copy-start | bytes 24580
  138.8 44.9 %copy-start.18 = (bf16[16,256]{1,0:T(8,128)(2,1)S(1)}, bf16[16,256]{1,0:T(8,128)(2,1)}, u32[]{:S(2)}) copy-start(bf16[16,256]{1,0:T(8,128)(2,1)} %get-tuple-element.56) | copy-start | bytes 24580
  143.5 23.8 %all-to-all-start.4 = ((f32[32,4,256]{2,1,0:T(4,128)}), f32[32,4,256]{2,1,0:T(4,128)S(1)}, u32[]{:S(2)}, u32[]{:S(2)}) async-start(f32[32,4,256]{2,1,0:T(4,128)} %bitcast.81), calls=%async_computation.4 | async-start | bytes 262144 | tf_op jit(solution)/shard_map/all_to_all | solution.py:292
  167.3 20.1 %copy-start.11 = (f32[32,4,256]{2,1,0:T(4,128)}, f32[32,4,256]{2,1,0:T(4,128)S(1)}, u32[]{:S(2)}) copy-start(f32[32,4,256]{2,1,0:T(4,128)S(1)} %all-to-all-done.4.slabs_ref) | copy-start | bytes 393220
  167.3 12.8 %all-to-all-start.2 = ((bf16[4,256,256]{2,1,0:T(8,128)(2,1)}), bf16[4,256,256]{2,1,0:T(8,128)(2,1)S(1)}, u32[]{:S(2)}, u32[]{:S(2)}) async-start(bf16[4,256,256]{2,1,0:T(8,128)(2,1)} %bitcast.67), calls=%async_computation.2 | async-start | bytes 1048576 | tf_op jit(solution)/shard_map/all_to_all | solution.py:287
  170.8 17.4 %copy-start.19 = (f32[4,256]{1,0:T(4,128)}, f32[4,256]{1,0:T(4,128)S(1)}, u32[]{:S(2)}) copy-start(f32[4,256]{1,0:T(4,128)S(1)} %fusion.28.onehot_ref) | copy-start | bytes 12292
  180.1 8.1 %copy-start.7 = (bf16[4,256,256]{2,1,0:T(8,128)(2,1)}, bf16[4,256,256]{2,1,0:T(8,128)(2,1)S(1)}, u32[]{:S(2)}) copy-start(bf16[4,256,256]{2,1,0:T(8,128)(2,1)S(1)} %all-to-all-done.2.first_ref) | copy-start | bytes 1572868
  180.1 8.1 %copy-start.13 = (f32[1,4,4,4]{1,2,3,0:T(4,128)S(1)}, f32[1,4,4,4]{1,2,3,0:T(4,128)}, u32[]{:S(2)}) copy-start(f32[1,4,4,4]{1,2,3,0:T(4,128)} %copy-done.12) | copy-start | bytes 772
  180.1 11.7 %all-to-all-start.3 = ((bf16[4,256,256]{2,1,0:T(8,128)(2,1)}), bf16[4,256,256]{2,1,0:T(8,128)(2,1)S(1)}, u32[]{:S(2)}, u32[]{:S(2)}) async-start(bf16[4,256,256]{2,1,0:T(8,128)(2,1)} %bitcast.288), calls=%async_computation.3 | async-start | bytes 1048576 | tf_op jit(solution)/shard_map/all_to_all | solution.py:287
  191.8 0.8 copy-start.8
Sparse Core Ops, SparseCore 0:
  9.9 84.4 all-gather.2

commit v3 on v2

v3 whole, which is shorter than its diff:
```python
import functools

import jax
import jax.numpy as jnp
from jax import lax
from jax.experimental import pallas as pl
from jax.experimental.pallas import tpu as pltpu
from jax.sharding import Mesh, PartitionSpec as P

CH = 256
NX, NZ, NY, NCORE = 4, 8, 4, 2
ROWS = 256
SLAB = 512
VMEM_LIMIT = 58 * 1024 * 1024
F32 = jnp.float32
BF16 = jnp.bfloat16
PRECISE = lax.Precision.HIGHEST


def system(site_decay, site_angle, site_mix):
    radius = 1.0 - site_decay
    norm_gain = jnp.sqrt(site_decay * (2.0 - site_decay))
    cos_ground = radius[0] * jnp.cos(site_angle[0])
    sin_ground = radius[0] * jnp.sin(site_angle[0])
    cos_high = radius[1] * jnp.cos(site_angle[1])
    sin_high = radius[1] * jnp.sin(site_angle[1])
    zeros_row = jnp.zeros_like(cos_ground)
    ones_row = jnp.ones_like(cos_ground)
    mix_a, mix_b, out_a, out_b = (site_mix[0], site_mix[1], site_mix[2], site_mix[3])
    row_list = [
        [cos_ground, -sin_ground, zeros_row, zeros_row],
        [sin_ground, cos_ground, zeros_row, zeros_row],
        [
            norm_gain[0] * (mix_a * cos_ground + mix_b * sin_ground),
            norm_gain[0] * (mix_b * cos_ground - mix_a * sin_ground),
            cos_high,
            -sin_high,
        ],
        [zeros_row, zeros_row, sin_high, cos_high],
    ]
    matrix = jnp.stack([jnp.stack(entries, axis=-1) for entries in row_list], axis=1)
    entry_vec = jnp.stack([ones_row, zeros_row, norm_gain[0] * mix_a, zeros_row], axis=-1)
    readout = jnp.stack([zeros_row, zeros_row, norm_gain[1] * out_a, norm_gain[1] * out_b], axis=-1)
    return (matrix, entry_vec, readout)


def tables(site_decay, site_angle, site_mix):
    matrix, entry_vec, readout = system(site_decay, site_angle, site_mix)
    classes = matrix.shape[0]
    powers = matrix[None]
    while powers.shape[0] < CH:
        further = jnp.einsum("kab,jkbc->jkac", powers[-1], powers, precision=PRECISE)
        powers = jnp.concatenate([powers, further], axis=0)
    gains = jnp.einsum("ka,jkab->kbj", readout, powers, precision=PRECISE)
    responses = jnp.einsum("jkab,kb->kja", powers[: CH - 1], entry_vec, precision=PRECISE)
    responses = jnp.concatenate([entry_vec[:, None, :], responses], axis=1)
    impulse = jnp.einsum("ka,kma->km", readout, responses, precision=PRECISE)
    padded_len = 2 * CH
    padded = jnp.concatenate([impulse, jnp.zeros((classes, CH), F32)], axis=1)
    tiled = jnp.tile(padded, (1, CH))[:, : CH * (padded_len - 1)]
    toeplitz = tiled.reshape(classes, CH, padded_len - 1)[:, :, :CH]
    toeplitz = toeplitz.reshape(classes * CH, CH).astype(BF16)
    final = responses[:, ::-1, :].transpose(0, 2, 1).astype(BF16)
    final = jnp.concatenate([final, jnp.zeros_like(final)], axis=1).reshape(classes * 8, CH)
    gains = gains.reshape(classes * 4, CH)
    gains_hi = lax.reduce_precision(gains, 8, 7)
    gains_lo = (gains - gains_hi).astype(BF16)
    gains_hi = gains_hi.astype(BF16)
    gain_stack = jnp.concatenate([gains_hi, gains_lo, gains_hi], axis=0)
    power = powers[-1]
    power_two = jnp.einsum("kab,kbc->kac", power, power, precision=PRECISE)
    return toeplitz, final, gain_stack, power, power_two


def per_row(power, onehot):
    return jnp.sum(power.transpose(2, 1, 0)[:, :, :, None] * onehot[None, None], axis=2)


def apply_power(table, state):
    out = table[0] * state[0:1]
    for b in range(1, 4):
        out = out + table[b] * state[b : b + 1]
    return out


def load(zs, where, g_ref, noise_refs, held, noise, sems):
    waits = []
    for b, z in enumerate(where):
        copies = []
        for q in range(NX):
            columns = pl.ds(pl.multiple_of(q * NZ * CH + zs[z] * CH, CH), CH)
            copies.append(
                pltpu.make_async_copy(
                    g_ref.at[pl.ds(q, NX - q), :, columns], held[q].at[b], sems.at[b, q]
                )
            )
        first = 0
        for j, ref in enumerate(noise_refs[b]):
            rows = pl.ds(first, ref.shape[0])
            copies.append(pltpu.make_async_copy(ref, noise.at[b, rows], sems.at[b, NX + j]))
            first += ref.shape[0]
        for copy in copies:
            copy.start()
        waits.append(copies)
    return waits


def term(held, noise, b, s):
    parts = [held[q][b, s - q] for q in range(s + 1)]
    rows = jnp.concatenate(parts, axis=1) if s else parts[0]
    return jnp.dot(rows, noise[b, 0 : (s + 1) * ROWS, :], preferred_element_type=F32)


def product_kernel(blocks, zs, g_ref, *refs):
    noise_refs, (out_ref, *held, noise, sems) = refs[:blocks], refs[blocks:]
    waits = load(zs, range(blocks), g_ref, [[r] for r in noise_refs], held, noise, sems)
    for b in range(blocks):
        for copy in waits[b]:
            copy.wait()
        for s in range(NX):
            rows = pl.ds(s * ROWS, ROWS)
            value = term(held, noise, b, s)
            out_ref[rows, :] = value if b == 0 else out_ref[rows, :] + value


def scratch(blocks):
    return [pltpu.VMEM((blocks, NX - q, ROWS, CH), BF16) for q in range(NX)] + [
        pltpu.VMEM((blocks, NX * ROWS, CH), BF16),
        pltpu.SemaphoreType.DMA((blocks, NX + 2)),
    ]


def whole(a):
    return pl.BlockSpec(a.shape, lambda i, zs: (0,) * len(a.shape))


ANYWHERE = pl.BlockSpec(memory_space=pl.ANY)


def product(gathered, where_z, noise_blocks):
    blocks = len(where_z)
    out = jax.ShapeDtypeStruct((NX * ROWS, CH), F32)
    return pl.pallas_call(
        functools.partial(product_kernel, blocks),
        grid_spec=pltpu.PrefetchScalarGridSpec(
            num_scalar_prefetch=1,
            grid=(1,),
            in_specs=[ANYWHERE] * (1 + blocks),
            out_specs=whole(out),
            scratch_shapes=scratch(blocks),
        ),
        out_shape=out,
        compiler_params=pltpu.CompilerParams(vmem_limit_bytes=VMEM_LIMIT),
        cost_estimate=pl.CostEstimate(
            flops=blocks * 2 * 10 * ROWS * CH * CH,
            bytes_accessed=blocks * (1310720 + 524288) + 1048576,
            transcendentals=0,
        ),
    )(jnp.stack(where_z).astype(jnp.int32), gathered, *noise_blocks)


def last_kernel(second, zs, g_ref, up_ref, down_ref, acc_ref, final_ref, onehot_ref, *refs):
    refs = list(refs)
    if second:
        end_ref, power_ref = refs.pop(0), refs.pop(0)
        piece_refs, send_ref = refs[:NX], refs[NX]
        refs = refs[NX + 1 :]
        local = refs.pop(0)
    else:
        local, end_out = refs.pop(0), refs.pop(0)
    *held, noise, sems = refs
    waits = load(zs, range(1), g_ref, [[up_ref, down_ref]], held, noise, sems)
    for copy in waits[0]:
        copy.wait()
    for s in range(NX):
        rows = pl.ds(s * ROWS, ROWS)
        local[rows, :] = (acc_ref[rows, :] + term(held, noise, 0, s)).astype(BF16)
    ends = lax.dot_general(
        final_ref[...], local[...], (((1,), (1,)), ((), ())), preferred_element_type=F32
    )
    picked = onehot_ref[0:1, :] * ends[0:4]
    for k in range(1, 4):
        picked = picked + onehot_ref[k : k + 1, :] * ends[k * 8 : k * 8 + 4]
    if not second:
        end_out[...] = picked
        return
    for d in range(NX):
        to = pl.multiple_of(lax.rem(zs[1] + d, NX) * ROWS, ROWS)
        piece_refs[d][...] = local[pl.ds(to, ROWS), :]
    slab_end = apply_power([power_ref[b] for b in range(4)], end_ref[...]) + picked
    for t in range(NY * NCORE * NX):
        block = t % NX
        send_ref[t] = slab_end[:, block * ROWS : (block + 1) * ROWS]


def last_product(scalars, gathered, up, down, acc, final, onehot, earlier=None):
    second = earlier is not None
    args = [acc, final, onehot] + (list(earlier) if second else [])
    if second:
        out_shape = [jax.ShapeDtypeStruct((ROWS, CH), BF16)] * NX
        out_shape.append(jax.ShapeDtypeStruct((NY * NCORE * NX, 4, ROWS), F32))
        extra = [pltpu.VMEM((NX * ROWS, CH), BF16)]
    else:
        out_shape = [
            jax.ShapeDtypeStruct((NX * ROWS, CH), BF16),
            jax.ShapeDtypeStruct((4, NX * ROWS), F32),
        ]
        extra = []
    return pl.pallas_call(
        functools.partial(last_kernel, second),
        grid_spec=pltpu.PrefetchScalarGridSpec(
            num_scalar_prefetch=1,
            grid=(1,),
            in_specs=[ANYWHERE] * 3 + [whole(a) for a in args],
            out_specs=[whole(a) for a in out_shape],
            scratch_shapes=extra + scratch(1),
        ),
        out_shape=out_shape,
        compiler_params=pltpu.CompilerParams(vmem_limit_bytes=VMEM_LIMIT),
        cost_estimate=pl.CostEstimate(
            flops=2 * 11 * ROWS * CH * CH, bytes_accessed=4 * 1048576, transcendentals=0
        ),
    )(scalars, gathered, up, down, *args)


def filter_kernel(
    place, first_ref, own_ref, by_one_ref, by_two_ref, by_three_ref, slabs_ref, mask_ref, onehot_ref, one_ref, two_ref,
    toeplitz_ref, final_ref, gain_ref, out_ref, state_ref, second_ref,
):
    step = pl.program_id(0)
    one = [one_ref[b] for b in range(4)]

    @pl.when(step == 0)
    def _():
        for d, ref in enumerate((own_ref, by_one_ref, by_two_ref, by_three_ref)):
            second_ref[lax.rem(place[1] + NX - d, NX)] = ref[...]
        two = [two_ref[b] for b in range(4)]

        def advance(t, state):
            return apply_power(two, state) + slabs_ref[t]

        state_ref[...] = lax.fori_loop(0, place[0], advance, jnp.zeros((4, ROWS), F32))

    state = state_ref[...]
    for half in range(2):
        local = second_ref[step] if half else first_ref[0]
        masked = jnp.concatenate([local * mask_ref[:, k : k + 1] for k in range(4)], axis=1)
        spread = jnp.concatenate([onehot_ref[k : k + 1, :] * state for k in range(4)], axis=0)
        high = spread.astype(BF16)
        low = (spread - high.astype(F32)).astype(BF16)
        stacked = jnp.concatenate([high, high, low], axis=0)
        carried = lax.dot_general(
            stacked, gain_ref[...], (((0,), (0,)), ((), ())), preferred_element_type=F32
        )
        out_ref[:, half * CH : (half + 1) * CH] = (
            jnp.dot(masked, toeplitz_ref[...], preferred_element_type=F32) + carried
        )
        ends = lax.dot_general(
            final_ref[...], local, (((1,), (1,)), ((), ())), preferred_element_type=F32
        )
        entered = onehot_ref[0:1, :] * ends[0:4]
        for k in range(1, 4):
            entered = entered + onehot_ref[k : k + 1, :] * ends[k * 8 : k * 8 + 4]
        state = apply_power(one, state) + entered
    state_ref[...] = state


def filtered(place, first, second, slabs, mask, onehot, one, two, toeplitz, final, gain):
    piece = pl.BlockSpec((1, ROWS, CH), lambda i, zs: (i, 0, 0))
    rest = (*second, slabs, mask, onehot, one, two, toeplitz, final, gain)
    return pl.pallas_call(
        filter_kernel,
        grid_spec=pltpu.PrefetchScalarGridSpec(
            num_scalar_prefetch=1,
            grid=(NX,),
            in_specs=[piece] + [whole(a) for a in rest],
            out_specs=pl.BlockSpec((ROWS, SLAB), lambda i, zs: (0, i)),
            scratch_shapes=[pltpu.VMEM((4, ROWS), F32), pltpu.VMEM((NX, ROWS, CH), BF16)],
        ),
        out_shape=jax.ShapeDtypeStruct((ROWS, NX * SLAB), F32),
        compiler_params=pltpu.CompilerParams(vmem_limit_bytes=VMEM_LIMIT),
        cost_estimate=pl.CostEstimate(
            flops=8 * 2 * ROWS * CH * 1100, bytes_accessed=4 * 1024 * 1024, transcendentals=0
        ),
    )(place, first, *rest)


def ring(value, by):
    return lax.ppermute(value, "z", [(i, (i + by) % NZ) for i in range(NZ)])


def body(factor, white_noise, site_class, site_decay, site_angle, site_mix):
    x = lax.axis_index("x")
    z = lax.axis_index("z")
    tm = lax.axis_index("y") * NCORE + lax.axis_index("c")

    share = lax.dynamic_slice(factor, (tm * 32, 0), (32, factor.shape[1]))
    gathered = lax.all_gather(share, ("x", "y", "c"), tiled=True)
    gathered = gathered.reshape(NX, ROWS, factor.shape[1])

    steps = []
    for half in range(2):
        first = half * CH
        slabs = jnp.concatenate(
            [white_noise[:, s * SLAB + first : s * SLAB + first + CH] for s in range(NX)], axis=0
        )
        own = lax.all_to_all(slabs, "x", 0, 0, tiled=True)
        up1, down1 = ring(own, 1), ring(own, -1)
        if half == 0:
            site_class, site_decay, site_angle, site_mix, up1 = lax.optimization_barrier(
                (site_class, site_decay, site_angle, site_mix, up1)
            )
        up2, down2 = ring(up1, 1), ring(down1, -1)
        up3, down3 = ring(up2, 1), ring(down2, -1)
        up4, down4 = ring(up3[:512], 1), ring(down3[512:], -1)
        steps.append(((own, up1, down1, up2, down2, up3, down3), up4, down4))

    toeplitz, final, gain, power, power_two = tables(site_decay, site_angle, site_mix)
    by_block = site_class.reshape(NX, NZ, ROWS)
    ids = jnp.arange(4, dtype=jnp.int32)
    tile_class = lax.dynamic_slice(by_block, (0, z, 0), (NX, 1, ROWS)).reshape(1, NX * ROWS)
    tile_hot = (tile_class == ids[:, None]).astype(F32)
    own_class = lax.dynamic_slice(by_block, (x, z, 0), (1, 1, ROWS)).reshape(1, ROWS)
    own_hot = (own_class == ids[:, None]).astype(F32)
    own_mask = (own_class.reshape(ROWS, 1) == ids[None, :]).astype(BF16)

    where_z = [(z + by) % NZ for by in (0, 7, 1, 6, 2, 5, 3)]
    scalars = jnp.stack([(z + 4) % NZ, x]).astype(jnp.int32)
    total = product(gathered, where_z, steps[0][0])
    local, end = last_product(
        scalars, gathered, steps[0][1], steps[0][2], total, final, tile_hot
    )
    first_part = lax.all_to_all(local, "x", 0, 0, tiled=True).reshape(NX, ROWS, CH)
    total = product(gathered, where_z, steps[1][0])
    first_part, total = lax.optimization_barrier((first_part, total))
    *pieces, to_send = last_product(
        scalars, gathered, steps[1][1], steps[1][2], total, final, tile_hot,
        (end, per_row(power, tile_hot)),
    )
    second_part = [pieces[0]] + [
        lax.ppermute(pieces[d], "x", [(i, (i + d) % NX) for i in range(NX)]) for d in (1, 2, 3)
    ]
    own_ends = lax.all_to_all(to_send, ("y", "c", "x"), 0, 0, tiled=True)
    return filtered(
        jnp.stack([tm * NX, x]).astype(jnp.int32),
        first_part, second_part, own_ends, own_mask, own_hot,
        per_row(power, own_hot), per_row(power_two, own_hot), toeplitz, final, gain,
    )


def solution(mesh):
    fine = Mesh(mesh.devices.reshape(NX, NZ, NY, NCORE), ("x", "z", "y", "c"))
    rows = ("x", "z")
    in_specs = (P(rows, None), P(rows, ("y", "c")), P(), P(), P(), P())
    return jax.shard_map(
        body, mesh=fine, in_specs=in_specs, out_specs=P(rows, ("y", "c")), check_vma=False
    )
```

time: 206 us -> 174 us (0.84)
  waiting for transfers between devices: 59.9 us -> 44.3 us
  starting transfers between devices: 53.1 us -> 39.5 us
  blocking collectives: 0 us -> 13.2 us
  Pallas kernels: 42.7 us -> 30.7 us
  other arithmetic: 8.37 us -> 6.18 us
    all_to_all x0 -> x1, blocking collectives: none -> 13.2 us  [body(): own = lax.all_to_all(slabs, 'x', 0, 0, tiled=True)]
    pallas_call x8 -> x4, Pallas kernels: 37.2 us -> 24.4 us  [the longest x2 14.8 us: product(): pl.pallas_call(functools.partial(product_kernel, blocks), grid_spec=pltpu...]
    all_to_all x2 -> x1, waiting for transfers between devices: 11.2 us -> 0.01 us  [body(): lax.all_to_all(local, 'x', 0, 0, tiled=True).reshape(NX, ROWS, CH)]
    ppermute x16, waiting for transfers between devices: 24.5 us -> 35.3 us  [ring(): return lax.ppermute(value, 'z', [(i, (i + by) % NZ) for i in range(NZ)])]
    all_to_all x2 -> x1, waiting for transfers between devices: 12.9 us -> 6.59 us  [body(): own = lax.all_to_all(slabs, 'x', 0, 0, tiled=True)]
    all_to_all x1, starting transfers between devices: 16.2 us -> 10.5 us  [body(): own_ends = lax.all_to_all(to_send, ('y', 'c', 'x'), 0, 0, tiled=True)]
    ppermute x0 -> x3, starting transfers between devices: none -> 5.06 us  [body(): lax.ppermute(pieces[d], 'x', [(i, (i + d) % NX) for i in range(NX)])]
    all_to_all x2 -> x1, starting transfers between devices: 8.33 us -> 3.48 us  [body(): own = lax.all_to_all(slabs, 'x', 0, 0, tiled=True)]
  transfers between devices with their start and end apart: 22 -> 23, of which waited for: 10 -> 10; matrix products, arithmetic and copies ran while one was open for 15% -> 16% of each run, Pallas kernels for 17% -> 11%
where the time goes in v3:
time: 174 us
  waiting for transfers between devices  44.3 us (25%)
  starting transfers between devices  39.5 us (23%)
  Pallas kernels  30.7 us (18%)
  local copies, waits for them, and re-layouts  19.6 us (11%)
  between operations  14 us (8%)
  blocking collectives  13.2 us (8%)
  other arithmetic  6.18 us (4%)
  matrix products  6.11 us (4%)
    ppermute x16, waiting for transfers between devices, ring(): return lax.ppermute(value, 'z', [(i, (i + by) % NZ) for i in range(NZ)])  35.3 us
    ppermute x16, starting transfers between devices, ring(): return lax.ppermute(value, 'z', [(i, (i + by) % NZ) for i in range(NZ)])  17 us
    pallas_call x2, Pallas kernels, product(): pl.pallas_call(functools.partial(product_kernel, blocks), grid_spec=pltpu...  14.8 us
    all_to_all x1, blocking collectives, body(): own = lax.all_to_all(slabs, 'x', 0, 0, tiled=True)  13.2 us
    all_to_all x1, starting transfers between devices, body(): own_ends = lax.all_to_all(to_send, ('y', 'c', 'x'), 0, 0, tiled=True)  10.5 us
    pallas_call x2, Pallas kernels, last_product(): pl.pallas_call(functools.partial(last_kernel, second), grid_spec=pltpu.Pr...  9.67 us
    all_to_all x1, waiting for transfers between devices, body(): own = lax.all_to_all(slabs, 'x', 0, 0, tiled=True)  6.59 us
    pallas_call x1, Pallas kernels, filtered(): pl.pallas_call(filter_kernel, grid_spec=pltpu.PrefetchScalarGridSpec(num_...  6.32 us
  transfers between devices with their start and end apart: 23, of which 10 were waited for; matrix products, arithmetic and copies ran while one was open for 16% of the time, Pallas kernels for 11%

profile of v3, /device:TPU:1, one launch (start us, length us, event | category | flops | bytes accessed | tf_op | source)
XLA Modules:
  0.0 173.6 jit_solution(3282579975313367195)
XLA Ops:
  6.5 1.9 %constant_dynamic-slice_fusion.2 = bf16[32,8192]{1,0:T(8,128)(2,1)} fusion(bf16[256,8192]{1,0:T(8,128)(2,1)} %param.6, s32[]{:T(128)S(6)} %select_n.46), kind=kLoop, calls=%fused_computation.65 | loop fusion | bytes 1048580 | tf_op jit(solution)/shard_map/dynamic_slice | solution.py:297
  8.5 1.4 fusion.36
  9.9 13.2 %all_to_all.36 = bf16[4,256,256]{2,1,0:T(8,128)(2,1)S(1)} all-to-all(bf16[4,256,256]{2,1,0:T(8,128)(2,1)S(1)} %bitcast.192), channel_id=1, replica_groups=mesh['x'=4,'z'=8,'y'=4,'c'=2] {'x'}, dimensions={0} | all-to-all | bytes 1048576 | tf_op jit(solution)/shard_map/all_to_all | solution.py:307
  23.1 1.7 collective-permute-start
  24.8 0.8 pad_maximum_fusion.1
  25.6 3.5 %all-to-all-start.2 = ((bf16[4,256,256]{2,1,0:T(8,128)(2,1)}), bf16[4,256,256]{2,1,0:T(8,128)(2,1)S(1)}, u32[]{:S(2)}, u32[]{:S(2)}) async-start(bf16[4,256,256]{2,1,0:T(8,128)(2,1)} %bitcast.67), calls=%async_computation.2 | async-start | bytes 1048576 | tf_op jit(solution)/shard_map/all_to_all | solution.py:307
  29.2 0.7 stack.106.zs
  30.4 0.6 pad_add_fusion.1.zs
  31.1 4.0 %collective-permute-start.4 = (bf16[1024,256]{1,0:T(8,128)(2,1)S(1)}, bf16[1024,256]{1,0:T(8,128)(2,1)}, u32[]{:S(2)}, u32[]{:S(2)}) collective-permute-start(bf16[1024,256]{1,0:T(8,128)(2,1)S(1)} %bitcast.190), channel_id=1, source_target_pairs={{0,56},{8,0},{16,8},{24,16},{32,24},{40,32},{48,40},{56,48},{1,57}... | collective-permute-start | bytes 1572872 | tf_op jit(solution)/shard_map/ppermute | solution.py:289
  35.0 6.6 %all-to-all-done.2 = bf16[4,256,256]{2,1,0:T(8,128)(2,1)S(1)} async-done(((bf16[4,256,256]{2,1,0:T(8,128)(2,1)}), bf16[4,256,256]{2,1,0:T(8,128)(2,1)S(1)}, u32[]{:S(2)}, u32[]{:S(2)}) %all-to-all-start.2) | async-done | bytes 524320 | tf_op jit(solution)/shard_map/all_to_all | solution.py:307
  41.9 2.8 %collective-permute-start.9 = (bf16[1024,256]{1,0:T(8,128)(2,1)S(1)}, bf16[1024,256]{1,0:T(8,128)(2,1)}, u32[]{:S(2)}, u32[]{:S(2)}) collective-permute-start(bf16[1024,256]{1,0:T(8,128)(2,1)S(1)} %bitcast.187), channel_id=1, source_target_pairs={{0,56},{8,0},{16,8},{24,16},{32,24},{40,32},{48,40},{56,48},{1,57}... | collective-permute-start | bytes 1572872 | tf_op jit(solution)/shard_map/ppermute | solution.py:289
  47.3 1.0 convolution_bitcast_fusion.4
  52.4 3.4 %fusion.38 = f32[4,1,256,4]{1,2,3,0:T(8,128)S(1)} fusion(f32[256,4,4,4]{0,2,3,1:T(4,128)S(1)} %concatenate.57, f32[4,4,1,1]{1,2,3,0:T(1,128)S(1)} %bitcast.207), kind=kOutput, calls=%fused_computation.92 | convolution fusion | flops 196608 | bytes 81984 | tf_op jit(solution)/shard_map/ka,jkab->kbj/dot_general | solution.py:54
  56.5 2.7 %collective-permute-start.5 = (bf16[1024,256]{1,0:T(8,128)(2,1)}, bf16[1024,256]{1,0:T(8,128)(2,1)}, u32[]{:S(2)}, u32[]{:S(2)}) collective-permute-start(bf16[1024,256]{1,0:T(8,128)(2,1)} %collective-permute-done.4.refs_2_), channel_id=1, source_target_pairs={{0,56},{8,0},{16,8},{24,16},{32,24},{40,32},{48,40},{56,48},{1,57}... | collective-permute-start | bytes 1572872 | tf_op jit(solution)/shard_map/ppermute | solution.py:289
  59.2 1.2 collective-permute-start.10
  60.4 1.4 collective-permute-start.11
  62.7 3.4 %collective-permute-done.1.refs_3_ = bf16[1024,256]{1,0:T(8,128)(2,1)} collective-permute-done((bf16[1024,256]{1,0:T(8,128)(2,1)}, bf16[1024,256]{1,0:T(8,128)(2,1)}, u32[]{:S(2)}, u32[]{:S(2)}) %collective-permute-start.1) | collective-permute-done | bytes 524320 | tf_op jit(solution)/shard_map/ppermute | solution.py:289
  66.0 4.2 %collective-permute-done.5.refs_4_ = bf16[1024,256]{1,0:T(8,128)(2,1)} collective-permute-done((bf16[1024,256]{1,0:T(8,128)(2,1)}, bf16[1024,256]{1,0:T(8,128)(2,1)}, u32[]{:S(2)}, u32[]{:S(2)}) %collective-permute-start.5) | collective-permute-done | bytes 524320 | tf_op jit(solution)/shard_map/ppermute | solution.py:289
  70.5 0.7 fusion.mask_ref
  71.3 6.0 %collective-permute-done.10.refs_3_ = bf16[1024,256]{1,0:T(8,128)(2,1)} collective-permute-done((bf16[1024,256]{1,0:T(8,128)(2,1)}, bf16[1024,256]{1,0:T(8,128)(2,1)}, u32[]{:S(2)}, u32[]{:S(2)}) %collective-permute-start.10) | collective-permute-done | bytes 524320 | tf_op jit(solution)/shard_map/ppermute | solution.py:289
  77.3 4.2 %collective-permute-done.11.refs_4_ = bf16[1024,256]{1,0:T(8,128)(2,1)} collective-permute-done((bf16[1024,256]{1,0:T(8,128)(2,1)}, bf16[1024,256]{1,0:T(8,128)(2,1)}, u32[]{:S(2)}, u32[]{:S(2)}) %collective-permute-start.11) | collective-permute-done | bytes 524320 | tf_op jit(solution)/shard_map/ppermute | solution.py:289
  81.5 7.0 %collective-permute-done.2.refs_5_ = bf16[1024,256]{1,0:T(8,128)(2,1)S(1)} collective-permute-done((bf16[1024,256]{1,0:T(8,128)(2,1)}, bf16[1024,256]{1,0:T(8,128)(2,1)S(1)}, u32[]{:S(2)}, u32[]{:S(2)}) %collective-permute-start.2) | collective-permute-done | bytes 524320 | tf_op jit(solution)/shard_map/ppermute | solution.py:289
  88.5 0.8 slice.137
  89.3 3.5 %collective-permute-done.6.refs_6_ = bf16[1024,256]{1,0:T(8,128)(2,1)} collective-permute-done((bf16[1024,256]{1,0:T(8,128)(2,1)}, bf16[1024,256]{1,0:T(8,128)(2,1)}, u32[]{:S(2)}, u32[]{:S(2)}) %collective-permute-start.6) | collective-permute-done | bytes 524320 | tf_op jit(solution)/shard_map/ppermute | solution.py:289
  92.8 1.7 slice.138
  95.1 7.4 %shard_map.64.acc_ref = f32[1024,256]{1,0:T(8,128)} custom-call(s32[7]{0:T(128)} %stack.106.zs, bf16[4,256,8192]{2,1,0:T(8,128)(2,1)} %bitcast.181, bf16[1024,256]{1,0:T(8,128)(2,1)} %bitcast.191, bf16[1024,256]{1,0:T(8,128)(2,1)} %collective-permute-done.refs_1_, bf16[1024,256]{1,0:T(8,128)(2,1)} %collective-permute-done.4.refs_2_, ...), custom_call_target="tpu_custom_call" | custom-call | flops 2348810240 | bytes 13893632 | tf_op jit(solution)/shard_map/pallas_call | solution.py:143
  102.4 2.8 %collective-permute-done.3.up_ref = bf16[512,256]{1,0:T(8,128)(2,1)S(1)} collective-permute-done((bf16[512,256]{1,0:T(8,128)(2,1)}, bf16[512,256]{1,0:T(8,128)(2,1)S(1)}, u32[]{:S(2)}, u32[]{:S(2)}) %collective-permute-start.3) | collective-permute-done | bytes 262176 | tf_op jit(solution)/shard_map/ppermute | solution.py:289
  105.3 4.2 %collective-permute-done.7.down_ref = bf16[512,256]{1,0:T(8,128)(2,1)S(1)} collective-permute-done((bf16[512,256]{1,0:T(8,128)(2,1)}, bf16[512,256]{1,0:T(8,128)(2,1)S(1)}, u32[]{:S(2)}, u32[]{:S(2)}) %collective-permute-start.7) | collective-permute-done | bytes 262176 | tf_op jit(solution)/shard_map/ppermute | solution.py:289
  109.5 0.7 copy-done.9
  110.2 4.8 %shard_map.65 = (bf16[1024,256]{1,0:T(8,128)(2,1)}, f32[4,1024]{1,0:T(4,128)}) custom-call(s32[2]{0:T(128)} %pad_add_fusion.1.zs, bf16[4,256,8192]{2,1,0:T(8,128)(2,1)} %bitcast.182, bf16[512,256]{1,0:T(8,128)(2,1)} %copy-done.8, bf16[512,256]{1,0:T(8,128)(2,1)} %copy-done.9, f32[1024,256]{1,0:T(8,128)} %shard_map.64.acc_ref, ...), custom_call_target="tpu_custom_call" | custom-call | flops 369098752 | bytes 4194304 | tf_op jit(solution)/shard_map/pallas_call | solution.py:209
  115.0 3.5 %all-to-all-start.1 = ((bf16[4,256,256]{2,1,0:T(8,128)(2,1)}), bf16[4,256,256]{2,1,0:T(8,128)(2,1)S(1)}, u32[]{:S(2)}, u32[]{:S(2)}) async-start(bf16[4,256,256]{2,1,0:T(8,128)(2,1)} %bitcast.193), calls=%async_computation.1 | async-start | bytes 1048576 | tf_op jit(solution)/shard_map/all_to_all | solution.py:333
  118.7 1.3 collective-permute-start.14
  120.0 0.8 slice.147
  120.8 1.5 collective-permute-start.15
  122.3 0.9 multiply_reduce_fusion.refs_1_
  123.1 7.4 %shard_map.66.acc_ref = f32[1024,256]{1,0:T(8,128)} custom-call(s32[7]{0:T(128)} %stack.106.zs, bf16[4,256,8192]{2,1,0:T(8,128)(2,1)} %bitcast.183, bf16[1024,256]{1,0:T(8,128)(2,1)} %bitcast.188, bf16[1024,256]{1,0:T(8,128)(2,1)} %collective-permute-done.8.refs_1_, bf16[1024,256]{1,0:T(8,128)(2,1)} %collective-permute-done.9.refs_2_, ...), custom_call_target="tpu_custom_call" | custom-call | flops 2348810240 | bytes 13893632 | tf_op jit(solution)/shard_map/pallas_call | solution.py:143
  130.6 0.8 copy-done.6
  131.4 4.9 %shard_map.67 = (bf16[256,256]{1,0:T(8,128)(2,1)}, bf16[256,256]{1,0:T(8,128)(2,1)}, bf16[256,256]{1,0:T(8,128)(2,1)}, bf16[256,256]{1,0:T(8,128)(2,1)}, f32[32,4,256]{2,1,0:T(4,128)}) custom-call(s32[2]{0:T(128)} %pad_add_fusion.1.zs, bf16[4,256,8192]{2,1,0:T(8,128)(2,1)} %bitcast.184, bf16[512,256]{1,0:T(8,128)(2,1)} %copy-done.6, ...), custom_call_target="tpu_custom_call" | custom-call | flops 369098752 | bytes 4194304 | tf_op jit(solution)/shard_map/pallas_call | solution.py:209
  136.3 1.6 collective-permute-start.16
  138.0 2.3 %collective-permute-start.17 = (bf16[256,256]{1,0:T(8,128)(2,1)}, bf16[256,256]{1,0:T(8,128)(2,1)S(1)}, u32[]{:S(2)}, u32[]{:S(2)}) collective-permute-start(bf16[256,256]{1,0:T(8,128)(2,1)} %get-tuple-element.30), channel_id=1, source_target_pairs={{0,128},{64,192},{128,0},{192,64},{1,129},{65,193},{129,1},{193,65... | collective-permute-start | bytes 393224 | tf_op jit(solution)/shard_map/ppermute | solution.py:341
  140.2 1.2 collective-permute-start.18
  141.4 10.5 %all-to-all-start.3 = ((f32[32,4,256]{2,1,0:T(4,128)}), f32[32,4,256]{2,1,0:T(4,128)S(1)}, u32[]{:S(2)}, u32[]{:S(2)}) async-start(f32[32,4,256]{2,1,0:T(4,128)} %get-tuple-element.32), calls=%async_computation.3 | async-start | bytes 262144 | tf_op jit(solution)/shard_map/all_to_all | solution.py:343
  152.7 0.8 copy.188
  153.9 1.8 %reshape.348 = bf16[4,256,511]{2,1,0:T(8,128)(2,1)S(1)} reshape(bf16[4,130816]{1,0:T(4,128)(2,1)S(1)} %slice.149) | data formatting | bytes 2093056 | tf_op jit(solution)/shard_map/reshape | solution.py:61
  155.6 0.8 slice.150
  156.5 0.8 multiply_reduce_fusion.1
  157.2 2.3 %all-to-all-done.3.slabs_ref = f32[32,4,256]{2,1,0:T(4,128)S(1)} async-done(((f32[32,4,256]{2,1,0:T(4,128)}), f32[32,4,256]{2,1,0:T(4,128)S(1)}, u32[]{:S(2)}, u32[]{:S(2)}) %all-to-all-start.3) | async-done | bytes 131104 | tf_op jit(solution)/shard_map/all_to_all | solution.py:343
  160.4 6.3 %shard_map.68 = f32[256,2048]{1,0:T(8,128)} custom-call(s32[2]{0:T(128)} %pad_add_fusion.place, bf16[4,256,256]{2,1,0:T(8,128)(2,1)} %copy-done.5, bf16[256,256]{1,0:T(8,128)(2,1)} %get-tuple-element.28.own_ref, bf16[256,256]{1,0:T(8,128)(2,1)} %copy-done.17, bf16[256,256]{1,0:T(8,128)(2,1)} %copy-done.18, bf16[256,256]{1,0:T(8,128)(2,1)} %copy-done.19, ...), custom_call_target="tpu_custom_call" | custom-call | flops 1153433600 | bytes 4194304 | tf_op jit(solution)/shard_map/pallas_call | solution.py:271
  (135 shorter events, 11.9 us)
Async XLA Ops:
  6.5 38.2 %copy-start.16 = (f32[2,4]{1,0:T(2,128)S(1)}, f32[2,4]{1,0:T(2,128)}, u32[]{:S(2)}) copy-start(f32[2,4]{1,0:T(2,128)} %param.9) | copy-start | bytes 100
  6.5 38.2 %copy-start.15 = (f32[2,4]{1,0:T(2,128)S(1)}, f32[2,4]{1,0:T(2,128)}, u32[]{:S(2)}) copy-start(f32[2,4]{1,0:T(2,128)} %param.10) | copy-start | bytes 100
  6.5 38.2 %copy-start.14 = (f32[4,4]{1,0:T(4,128)S(1)}, f32[4,4]{1,0:T(4,128)}, u32[]{:S(2)}) copy-start(f32[4,4]{1,0:T(4,128)} %param.11) | copy-start | bytes 196
  6.5 88.5 %all-gather.2.cloned.1.call-start = ((), (), s32[]{:S(2)}) async-start(), calls=%async_computation.4 | async-start | bytes 17301504 | tf_op jit(solution)/shard_map/all_gather | solution.py:298
  9.8 42.1 %copy-start.12 = (s32[8192]{0:T(1024)S(1)}, s32[8192]{0:T(1024)}, u32[]{:S(2)}) copy-start(s32[8192]{0:T(1024)} %param.8) | copy-start | bytes 98308
  23.1 33.4 %copy-start.1 = (bf16[4,256,256]{2,1,0:T(8,128)(2,1)}, bf16[4,256,256]{2,1,0:T(8,128)(2,1)S(1)}, u32[]{:S(2)}) copy-start(bf16[4,256,256]{2,1,0:T(8,128)(2,1)S(1)} %all_to_all.36) | copy-start | bytes 1572868
  23.1 21.6 %collective-permute-start = (bf16[1024,256]{1,0:T(8,128)(2,1)S(1)}, bf16[1024,256]{1,0:T(8,128)(2,1)}, u32[]{:S(2)}, u32[]{:S(2)}) collective-permute-start(bf16[1024,256]{1,0:T(8,128)(2,1)S(1)} %bitcast.189), channel_id=1, source_target_pairs={{0,8},{8,16},{16,24},{24,32},{32,40},{40,48},{48,56},{56,0},{1,9},... | collective-permute-start | bytes 1572872 | tf_op jit(solution)/shard_map/ppermute | solution.py:289
  25.6 16.0 %all-to-all-start.2 = ((bf16[4,256,256]{2,1,0:T(8,128)(2,1)}), bf16[4,256,256]{2,1,0:T(8,128)(2,1)S(1)}, u32[]{:S(2)}, u32[]{:S(2)}) async-start(bf16[4,256,256]{2,1,0:T(8,128)(2,1)} %bitcast.67), calls=%async_computation.2 | async-start | bytes 1048576 | tf_op jit(solution)/shard_map/all_to_all | solution.py:307
  31.1 25.4 %collective-permute-start.4 = (bf16[1024,256]{1,0:T(8,128)(2,1)S(1)}, bf16[1024,256]{1,0:T(8,128)(2,1)}, u32[]{:S(2)}, u32[]{:S(2)}) collective-permute-start(bf16[1024,256]{1,0:T(8,128)(2,1)S(1)} %bitcast.190), channel_id=1, source_target_pairs={{0,56},{8,0},{16,8},{24,16},{32,24},{40,32},{48,40},{56,48},{1,57}... | collective-permute-start | bytes 1572872 | tf_op jit(solution)/shard_map/ppermute | solution.py:289
  41.6 29.7 %copy-start = (bf16[4,256,256]{2,1,0:T(8,128)(2,1)}, bf16[4,256,256]{2,1,0:T(8,128)(2,1)S(1)}, u32[]{:S(2)}) copy-start(bf16[4,256,256]{2,1,0:T(8,128)(2,1)S(1)} %all-to-all-done.2) | copy-start | bytes 1572868
  41.6 17.6 %collective-permute-start.8 = (bf16[1024,256]{1,0:T(8,128)(2,1)S(1)}, bf16[1024,256]{1,0:T(8,128)(2,1)}, u32[]{:S(2)}, u32[]{:S(2)}) collective-permute-start(bf16[1024,256]{1,0:T(8,128)(2,1)S(1)} %bitcast.186), channel_id=1, source_target_pairs={{0,8},{8,16},{16,24},{24,32},{32,40},{40,48},{48,56},{56,0},{1,9},... | collective-permute-start | bytes 1572872 | tf_op jit(solution)/shard_map/ppermute | solution.py:289
  41.9 18.6 %collective-permute-start.9 = (bf16[1024,256]{1,0:T(8,128)(2,1)S(1)}, bf16[1024,256]{1,0:T(8,128)(2,1)}, u32[]{:S(2)}, u32[]{:S(2)}) collective-permute-start(bf16[1024,256]{1,0:T(8,128)(2,1)S(1)} %bitcast.187), channel_id=1, source_target_pairs={{0,56},{8,0},{16,8},{24,16},{32,24},{40,32},{48,40},{56,48},{1,57}... | collective-permute-start | bytes 1572872 | tf_op jit(solution)/shard_map/ppermute | solution.py:289
  50.7 15.3 %collective-permute-start.1 = (bf16[1024,256]{1,0:T(8,128)(2,1)}, bf16[1024,256]{1,0:T(8,128)(2,1)}, u32[]{:S(2)}, u32[]{:S(2)}) collective-permute-start(bf16[1024,256]{1,0:T(8,128)(2,1)} %collective-permute-done.refs_1_), channel_id=1, source_target_pairs={{0,8},{8,16},{16,24},{24,32},{32,40},{40,48},{48,56},{56,0},{1,9},... | collective-permute-start | bytes 1572872 | tf_op jit(solution)/shard_map/ppermute | solution.py:289
  56.5 13.8 %collective-permute-start.5 = (bf16[1024,256]{1,0:T(8,128)(2,1)}, bf16[1024,256]{1,0:T(8,128)(2,1)}, u32[]{:S(2)}, u32[]{:S(2)}) collective-permute-start(bf16[1024,256]{1,0:T(8,128)(2,1)} %collective-permute-done.4.refs_2_), channel_id=1, source_target_pairs={{0,56},{8,0},{16,8},{24,16},{32,24},{40,32},{48,40},{56,48},{1,57}... | collective-permute-start | bytes 1572872 | tf_op jit(solution)/shard_map/ppermute | solution.py:289
  59.2 18.1 %collective-permute-start.10 = (bf16[1024,256]{1,0:T(8,128)(2,1)}, bf16[1024,256]{1,0:T(8,128)(2,1)}, u32[]{:S(2)}, u32[]{:S(2)}) collective-permute-start(bf16[1024,256]{1,0:T(8,128)(2,1)} %collective-permute-done.8.refs_1_), channel_id=1, source_target_pairs={{0,8},{8,16},{16,24},{24,32},{32,40},{40,48},{48,56},{56,0},{1,9},... | collective-permute-start | bytes 1572872 | tf_op jit(solution)/shard_map/ppermute | solution.py:289
  60.4 21.1 %collective-permute-start.11 = (bf16[1024,256]{1,0:T(8,128)(2,1)}, bf16[1024,256]{1,0:T(8,128)(2,1)}, u32[]{:S(2)}, u32[]{:S(2)}) collective-permute-start(bf16[1024,256]{1,0:T(8,128)(2,1)} %collective-permute-done.9.refs_2_), channel_id=1, source_target_pairs={{0,56},{8,0},{16,8},{24,16},{32,24},{40,32},{48,40},{56,48},{1,57}... | collective-permute-start | bytes 1572872 | tf_op jit(solution)/shard_map/ppermute | solution.py:289
  66.0 22.5 %collective-permute-start.2 = (bf16[1024,256]{1,0:T(8,128)(2,1)}, bf16[1024,256]{1,0:T(8,128)(2,1)S(1)}, u32[]{:S(2)}, u32[]{:S(2)}) collective-permute-start(bf16[1024,256]{1,0:T(8,128)(2,1)} %collective-permute-done.1.refs_3_), channel_id=1, source_target_pairs={{0,8},{8,16},{16,24},{24,32},{32,40},{40,48},{48,56},{56,0},{1,9},... | collective-permute-start | bytes 1572872 | tf_op jit(solution)/shard_map/ppermute | solution.py:289
  70.3 22.5 %collective-permute-start.6 = (bf16[1024,256]{1,0:T(8,128)(2,1)}, bf16[1024,256]{1,0:T(8,128)(2,1)}, u32[]{:S(2)}, u32[]{:S(2)}) collective-permute-start(bf16[1024,256]{1,0:T(8,128)(2,1)} %collective-permute-done.5.refs_4_), channel_id=1, source_target_pairs={{0,56},{8,0},{16,8},{24,16},{32,24},{40,32},{48,40},{56,48},{1,57}... | collective-permute-start | bytes 1572872 | tf_op jit(solution)/shard_map/ppermute | solution.py:289
  77.3 41.4 %collective-permute-start.12 = (bf16[1024,256]{1,0:T(8,128)(2,1)}, bf16[1024,256]{1,0:T(8,128)(2,1)S(1)}, u32[]{:S(2)}, u32[]{:S(2)}) collective-permute-start(bf16[1024,256]{1,0:T(8,128)(2,1)} %collective-permute-done.10.refs_3_), channel_id=1, source_target_pairs={{0,8},{8,16},{16,24},{24,32},{32,40},{40,48},{48,56},{56,0},{1,9},... | collective-permute-start | bytes 1572872 | tf_op jit(solution)/shard_map/ppermute | solution.py:289
  81.5 38.5 %collective-permute-start.13 = (bf16[1024,256]{1,0:T(8,128)(2,1)}, bf16[1024,256]{1,0:T(8,128)(2,1)S(1)}, u32[]{:S(2)}, u32[]{:S(2)}) collective-permute-start(bf16[1024,256]{1,0:T(8,128)(2,1)} %collective-permute-done.11.refs_4_), channel_id=1, source_target_pairs={{0,56},{8,0},{16,8},{24,16},{32,24},{40,32},{48,40},{56,48},{1,57}... | collective-permute-start | bytes 1572872 | tf_op jit(solution)/shard_map/ppermute | solution.py:289
  88.5 6.5 %copy-start.4 = (bf16[1024,256]{1,0:T(8,128)(2,1)}, bf16[1024,256]{1,0:T(8,128)(2,1)S(1)}, u32[]{:S(2)}) copy-start(bf16[1024,256]{1,0:T(8,128)(2,1)S(1)} %collective-permute-done.2.refs_5_) | copy-start | bytes 1572868
  89.3 16.0 %collective-permute-start.3 = (bf16[512,256]{1,0:T(8,128)(2,1)}, bf16[512,256]{1,0:T(8,128)(2,1)S(1)}, u32[]{:S(2)}, u32[]{:S(2)}) collective-permute-start(bf16[512,256]{1,0:T(8,128)(2,1)} %slice.137), channel_id=1, source_target_pairs={{0,8},{8,16},{16,24},{24,32},{32,40},{40,48},{48,56},{56,0},{1,9},... | collective-permute-start | bytes 786440 | tf_op jit(solution)/shard_map/ppermute | solution.py:289
  94.4 15.1 %collective-permute-start.7 = (bf16[512,256]{1,0:T(8,128)(2,1)}, bf16[512,256]{1,0:T(8,128)(2,1)S(1)}, u32[]{:S(2)}, u32[]{:S(2)}) collective-permute-start(bf16[512,256]{1,0:T(8,128)(2,1)} %slice.138), channel_id=1, source_target_pairs={{0,56},{8,0},{16,8},{24,16},{32,24},{40,32},{48,40},{56,48},{1,57}... | collective-permute-start | bytes 786440 | tf_op jit(solution)/shard_map/ppermute | solution.py:289
  102.4 19.8 %copy-start.10 = (f32[4,1024]{1,0:T(4,128)S(1)}, f32[4,1024]{1,0:T(4,128)}, u32[]{:S(2)}) copy-start(f32[4,1024]{1,0:T(4,128)} %fusion.13.onehot_ref) | copy-start | bytes 49156
  105.3 4.2 %copy-start.8 = (bf16[512,256]{1,0:T(8,128)(2,1)}, bf16[512,256]{1,0:T(8,128)(2,1)S(1)}, u32[]{:S(2)}) copy-start(bf16[512,256]{1,0:T(8,128)(2,1)S(1)} %collective-permute-done.3.up_ref) | copy-start | bytes 786436
  109.5 0.7 copy-start.9
  115.0 15.5 %all-to-all-start.1 = ((bf16[4,256,256]{2,1,0:T(8,128)(2,1)}), bf16[4,256,256]{2,1,0:T(8,128)(2,1)S(1)}, u32[]{:S(2)}, u32[]{:S(2)}) async-start(bf16[4,256,256]{2,1,0:T(8,128)(2,1)} %bitcast.193), calls=%async_computation.1 | async-start | bytes 1048576 | tf_op jit(solution)/shard_map/all_to_all | solution.py:333
  118.5 38.0 %copy-start.13 = (f32[4,256]{1,0:T(4,128)}, f32[4,256]{1,0:T(4,128)S(1)}, u32[]{:S(2)}) copy-start(f32[4,256]{1,0:T(4,128)S(1)} %fusion.20.onehot_ref) | copy-start | bytes 12292
  118.7 4.4 %copy-start.2 = (bf16[1024,256]{1,0:T(8,128)(2,1)}, bf16[1024,256]{1,0:T(8,128)(2,1)S(1)}, u32[]{:S(2)}) copy-start(bf16[1024,256]{1,0:T(8,128)(2,1)S(1)} %collective-permute-done.12.refs_5_) | copy-start | bytes 1572868
  118.7 11.8 %collective-permute-start.14 = (bf16[512,256]{1,0:T(8,128)(2,1)S(1)}, bf16[512,256]{1,0:T(8,128)(2,1)S(1)}, u32[]{:S(2)}, u32[]{:S(2)}) collective-permute-start(bf16[512,256]{1,0:T(8,128)(2,1)S(1)} %slice.146), channel_id=1, source_target_pairs={{0,8},{8,16},{16,24},{24,32},{32,40},{40,48},{48,56},{56,0},{1,9},... | collective-permute-start | bytes 786440 | tf_op jit(solution)/shard_map/ppermute | solution.py:289
  120.0 3.1 %copy-start.3 = (bf16[1024,256]{1,0:T(8,128)(2,1)}, bf16[1024,256]{1,0:T(8,128)(2,1)S(1)}, u32[]{:S(2)}) copy-start(bf16[1024,256]{1,0:T(8,128)(2,1)S(1)} %collective-permute-done.13.refs_6_) | copy-start | bytes 1572868
  120.8 9.8 %collective-permute-start.15 = (bf16[512,256]{1,0:T(8,128)(2,1)}, bf16[512,256]{1,0:T(8,128)(2,1)S(1)}, u32[]{:S(2)}, u32[]{:S(2)}) collective-permute-start(bf16[512,256]{1,0:T(8,128)(2,1)} %slice.147), channel_id=1, source_target_pairs={{0,56},{8,0},{16,8},{24,16},{32,24},{40,32},{48,40},{56,48},{1,57}... | collective-permute-start | bytes 786440 | tf_op jit(solution)/shard_map/ppermute | solution.py:289
  130.5 5.8 %copy-start.5 = (bf16[4,256,256]{2,1,0:T(8,128)(2,1)}, bf16[4,256,256]{2,1,0:T(8,128)(2,1)S(1)}, u32[]{:S(2)}) copy-start(bf16[4,256,256]{2,1,0:T(8,128)(2,1)S(1)} %all-to-all-done.1.first_ref) | copy-start | bytes 1572868
  130.6 0.8 copy-start.6
  130.6 0.9 copy-start.7
  136.3 23.2 %collective-permute-start.16 = (bf16[256,256]{1,0:T(8,128)(2,1)}, bf16[256,256]{1,0:T(8,128)(2,1)S(1)}, u32[]{:S(2)}, u32[]{:S(2)}) collective-permute-start(bf16[256,256]{1,0:T(8,128)(2,1)} %get-tuple-element.29), channel_id=1, source_target_pairs={{0,64},{64,128},{128,192},{192,0},{1,65},{65,129},{129,193},{193,1... | collective-permute-start | bytes 393224 | tf_op jit(solution)/shard_map/ppermute | solution.py:341
  138.0 21.6 %collective-permute-start.17 = (bf16[256,256]{1,0:T(8,128)(2,1)}, bf16[256,256]{1,0:T(8,128)(2,1)S(1)}, u32[]{:S(2)}, u32[]{:S(2)}) collective-permute-start(bf16[256,256]{1,0:T(8,128)(2,1)} %get-tuple-element.30), channel_id=1, source_target_pairs={{0,128},{64,192},{128,0},{192,64},{1,129},{65,193},{129,1},{193,65... | collective-permute-start | bytes 393224 | tf_op jit(solution)/shard_map/ppermute | solution.py:341
  140.2 19.4 %collective-permute-start.18 = (bf16[256,256]{1,0:T(8,128)(2,1)}, bf16[256,256]{1,0:T(8,128)(2,1)S(1)}, u32[]{:S(2)}, u32[]{:S(2)}) collective-permute-start(bf16[256,256]{1,0:T(8,128)(2,1)} %get-tuple-element.31), channel_id=1, source_target_pairs={{0,192},{64,0},{128,64},{192,128},{1,193},{65,1},{129,65},{193,129... | collective-permute-start | bytes 393224 | tf_op jit(solution)/shard_map/ppermute | solution.py:341
  141.4 18.2 %all-to-all-start.3 = ((f32[32,4,256]{2,1,0:T(4,128)}), f32[32,4,256]{2,1,0:T(4,128)S(1)}, u32[]{:S(2)}, u32[]{:S(2)}) async-start(f32[32,4,256]{2,1,0:T(4,128)} %get-tuple-element.32), calls=%async_computation.3 | async-start | bytes 262144 | tf_op jit(solution)/shard_map/all_to_all | solution.py:343
  159.6 0.7 copy-start.11
  159.6 0.7 copy-start.17
  159.6 0.8 copy-start.18
  159.6 0.8 copy-start.19
Sparse Core Ops, SparseCore 0:
  9.9 84.2 all-gather.1
